TPU v7x, 512 devices: a whole 4x8x8 slice. The times are simulated.
512 devices in a mesh: gx: 8 (over x, core), gy: 8 (over z), vert: 8 (over y).
Axes of the slice: x: 4, y: 8, z: 8, core: 2. Of those that a mesh axis runs over, the one named last changes fastest.
Arguments:
- distribution: bfloat16 [64, 16, 24, 4608], P('gx', 'gy', 'vert'), may hold values from 0.049804688 to 2
- wall_mask: int32 [64, 16], replicated, may hold values from 0 to 2
- pair_table: int32 [8, 8], replicated, may hold values from 0 to 7
- trans_weight: float32 [8], replicated, may hold values from 0.02 to 0.25
- kernels: float32 [5, 13824], replicated, as said below
Outputs:
- new_distribution: bfloat16 [64, 16, 24, 4608], P('gx', 'gy', 'vert')
Inputs may be any that keep to these rules, and one draw needn't show every extreme that they name: `wall_mask`: 0 marks a fluid cell, 1 a solid cell, 2 a cut cell at the wall. `pair_table`: indexes trans_weight. `kernels`: every entry is positive, and each row is even in each mode index separately: unchanged when the x mode a becomes (24 - a) mod 24, and likewise for the y and z modes.
All inputs are finite; a program needn't handle non-finite values.
Results may differ from a plain program's by a relative error of at most 0.001.
The roundings to bfloat16 on the way count: a program that leaves them out, or rounds other values in their place, can miss the bound.
Values may be sent and summed in bfloat16 or wider, within the bound.
No kernel may reach another device: no remote copies, remote signals or barrier semaphores. Data moves between devices by JAX's collectives and lax.ppermute only.
A program may use at most 64 MiB of HBM per device.

v0:
```python
import math

import numpy as np
import jax
import jax.numpy as jnp
from jax import lax
from jax.experimental import pallas as pl
from jax.experimental.pallas import tpu as pltpu
from jax.sharding import PartitionSpec as P

VX = 24
VY = 24
VZ = 24
LEVELS = 8
PLANE = VY * VZ
HALF = PLANE // 2
SUB = 3
LANES = SUB * HALF
WIDE = 896

courant = 0.45
collide_step = 0.4
high = lax.Precision.HIGH


def open_share(wall_mask):
    return jnp.where(wall_mask == 1, 0.0, jnp.where(wall_mask == 2, 0.5, 1.0)).astype(jnp.float32)


def cas_matrix(extent):
    counter = np.arange(extent)
    angles = (np.outer(counter, counter) % extent) * (2.0 * np.pi / extent)
    return np.cos(angles) + np.sin(angles)


def speed(index):
    return courant * (2.0 * index - (VX - 1)) / (VX - 1)


def lane_speeds():
    rows = []
    for half in range(2):
        j = np.arange(HALF) // VZ + half * (VY // 2)
        row = np.zeros((WIDE,), np.float32)
        row[:LANES] = np.tile(np.abs(speed(j)), SUB)
        rows.append(np.broadcast_to(row, (LEVELS, WIDE)))
    return np.stack(rows).astype(np.float32)


def minmod(a, b):
    return jnp.maximum(jnp.minimum(a, b), jnp.minimum(jnp.maximum(a, b), 0.0))


def transport_kernel(flags, face_x, face_y, own, xup, xdn, low, high_, speeds_x, speeds_y, out):
    rows_x = own.shape[1]
    forward = flags[0] > 0

    def pick(step):
        return jnp.where(forward, step, rows_x - 1 - step)

    def tile(t, carry):
        lanes = pl.ds(pl.multiple_of(t * 128, 128), 128)
        nu_x = speeds_x[:, lanes]
        half_x = 0.5 * (1.0 - nu_x)
        for half in range(2):
            nu_y = speeds_y[half, :, lanes]
            half_y = 0.5 * (1.0 - nu_y)
            first, second = (0, 1) if half == 1 else (1, 0)

            def f32(ref, *at):
                return ref[at[0], at[1], :, lanes].astype(jnp.float32)

            prev = []
            for y in range(2):
                q = 2 * y + half
                far = f32(xup, q, 0)
                near = f32(xup, q, 1)
                now = f32(own, q, pick(0))
                slope = minmod(near - far, now - near)
                flux = face_x[0, y] * (nu_x * (near + half_x * slope))
                prev.append((now, now - near, flux))
            for step in range(rows_x):
                row = pick(step)
                changed = []
                values = []
                for y in range(2):
                    q = 2 * y + half
                    now, diff, flux = prev[y]
                    if step + 1 < rows_x:
                        nxt = f32(own, q, pick(step + 1))
                    else:
                        nxt = f32(xdn, q, 0)
                    later = nxt - now
                    flux_out = face_x[step + 1, y] * (
                        nu_x * (now + half_x * minmod(diff, later))
                    )
                    changed.append(now + (flux - flux_out))
                    values.append(now)
                    prev[y] = (nxt, later, flux_out)
                if half == 1:
                    up2, up1, down = f32(low, 0, row), f32(low, 1, row), f32(high_, 2, row)
                else:
                    up2, up1, down = f32(high_, 1, row), f32(high_, 0, row), f32(low, 2, row)
                a, b = values[first], values[second]
                d0, d1, d2, d3 = up1 - up2, a - up1, b - a, down - b
                w0, w1, w2 = (0, 1, 2) if half == 1 else (2, 1, 0)
                g0 = face_y[row, w0] * (nu_y * (up1 + half_y * minmod(d0, d1)))
                g1 = face_y[row, w1] * (nu_y * (a + half_y * minmod(d1, d2)))
                g2 = face_y[row, w2] * (nu_y * (b + half_y * minmod(d2, d3)))
                out[row, 2 * first + half, :, lanes] = (changed[first] + (g0 - g1)).astype(
                    jnp.bfloat16
                )
                out[row, 2 * second + half, :, lanes] = (changed[second] + (g1 - g2)).astype(
                    jnp.bfloat16
                )
        return carry

    lax.fori_loop(0, WIDE // 128, tile, 0)


def transport(flag, face_x, face_y, own, xup, xdn, low, high_, speeds_x, speeds_y):
    rows_x = own.shape[1]
    smem = pl.BlockSpec(memory_space=pltpu.SMEM)
    vmem = pl.BlockSpec(memory_space=pltpu.VMEM)
    return pl.pallas_call(
        transport_kernel,
        out_shape=jax.ShapeDtypeStruct((rows_x, 4, LEVELS, WIDE), jnp.bfloat16),
        in_specs=[smem] * 3 + [vmem] * 7,
        out_specs=vmem,
        compiler_params=pltpu.CompilerParams(vmem_limit_bytes=32 * 1024 * 1024),
        cost_estimate=pl.CostEstimate(flops=10_000_000, bytes_accessed=2_000_000, transcendentals=0),
    )(flag, face_x, face_y, own, xup, xdn, low, high_, speeds_x, speeds_y)


def transform(fields, table_x, table_yz):
    partial_x = jnp.einsum("ab,nblc->nalc", table_x, fields, precision=high)
    return jnp.einsum("nalc,cd->nald", partial_x, table_yz, precision=high)


def ring(count, step):
    return [(i, (i + step) % count) for i in range(count)]


def body(distribution, wall_mask, pair_table, trans_weight, kernels):
    rows_x, rows_y, local_vx, row_width = distribution.shape
    count_x = lax.axis_size("gx")
    count_y = lax.axis_size("gy")
    count_v = lax.axis_size("vert")
    at_v = lax.axis_index("vert")
    forward = at_v >= count_v // 2

    own = distribution.reshape(rows_x, 2, SUB, LEVELS, 2, HALF)
    own = own.transpose(1, 4, 0, 3, 2, 5).reshape(4, rows_x, LEVELS, LANES)
    own = jnp.pad(own, ((0, 0), (0, 0), (0, 0), (0, WIDE - LANES)))

    low = lax.ppermute(jnp.stack([own[1], own[3], own[2]]), "gy", ring(count_y, 1))
    high_ = lax.ppermute(jnp.stack([own[0], own[2], own[1]]), "gy", ring(count_y, -1))
    upstream = jnp.where(forward, own[:, rows_x - 2 :], own[:, 1::-1])
    downstream = jnp.where(forward, own[:, :1], own[:, rows_x - 1 :])
    send_up, send_down = [], []
    for i in range(count_x):
        for v in range(count_v):
            step = 1 if v >= count_v // 2 else -1
            send_up.append((i * count_v + v, (i + step) % count_x * count_v + v))
            send_down.append((i * count_v + v, (i - step) % count_x * count_v + v))
    xup = lax.ppermute(upstream, ("gx", "vert"), send_up)
    xdn = lax.ppermute(downstream, ("gx", "vert"), send_down)

    openness = open_share(wall_mask)
    wrapped = jnp.pad(openness, 1, mode="wrap")
    anchor_x = lax.axis_index("gx") * rows_x
    anchor_y = lax.axis_index("gy") * rows_y
    window = lax.dynamic_slice(wrapped, (anchor_x, anchor_y), (rows_x + 2, rows_y + 2))
    open_x = window[:, 1 : rows_y + 1]
    face_x = jnp.minimum(open_x[:-1], open_x[1:])
    face_x = jnp.where(forward, face_x, face_x[::-1])
    open_y = window[1 : rows_x + 1]
    face_y = jnp.minimum(open_y[:, :-1], open_y[:, 1:])
    own_open = lax.dynamic_slice(openness, (anchor_x + at_v, anchor_y), (1, rows_y))[0]

    index_x = at_v * local_vx + jnp.arange(WIDE, dtype=jnp.int32) // HALF
    speeds_x = jnp.abs(speed(index_x.astype(jnp.float32)))
    speeds_x = jnp.broadcast_to(speeds_x[None], (LEVELS, WIDE))
    speeds_y = jnp.asarray(lane_speeds())
    flag = forward.astype(jnp.int32).reshape(1)
    transported = transport(flag, face_x, face_y, own, xup, xdn, low, high_, speeds_x, speeds_y)

    block = lax.all_to_all(transported, "vert", split_axis=0, concat_axis=0, tiled=True)
    fields = block[..., :LANES].reshape(count_v, 2, 2, LEVELS, SUB, HALF)
    fields = fields.transpose(1, 0, 4, 3, 2, 5).reshape(2, VX, LEVELS, PLANE).astype(jnp.float32)

    entries = jnp.arange(trans_weight.shape[0], dtype=jnp.int32)
    mixing = jnp.sum(
        jnp.where(
            pair_table[:, :, None] == entries[None, None, :], trans_weight[None, None, :], 0.0
        ),
        axis=-1,
    )
    table_x = jnp.asarray(cas_matrix(VX).astype(np.float32))
    table_yz = jnp.asarray(np.kron(cas_matrix(VY), cas_matrix(VZ)).astype(np.float32))
    bank = kernels.reshape(kernels.shape[0], VX, 1, PLANE) / float(VX * PLANE)
    spectrum = transform(fields, table_x, table_yz)
    mixed_spectrum = jnp.einsum("lm,namc->nalc", mixing, spectrum, precision=high)
    gain_term = jnp.zeros_like(fields)
    for direction in range(2):
        gain_left = transform(bank[direction] * spectrum, table_x, table_yz)
        gain_right = transform(bank[2 + direction] * mixed_spectrum, table_x, table_yz)
        gain_term = gain_term + gain_left * gain_right
    loss_term = transform(bank[4] * mixed_spectrum, table_x, table_yz)
    collision = gain_term - fields * loss_term
    weights = own_open.reshape(2, 1, 1, 1)
    updated = (fields + collide_step * weights * collision).astype(jnp.bfloat16)
    updated = updated.reshape(1, 2, VX, row_width)
    return lax.all_to_all(updated, "vert", split_axis=2, concat_axis=0, tiled=True)


def solution(mesh):
    in_specs = (P("gx", "gy", "vert", None), P(), P(), P(), P())
    out_specs = P("gx", "gy", "vert", None)
    return jax.shard_map(body, mesh=mesh, in_specs=in_specs, out_specs=out_specs, check_vma=False)
```

profile of v0, /device:TPU:7, one launch (start us, length us, event | category | flops | bytes accessed | tf_op | source)
XLA Modules:
  0.0 94.5 jit_solution(532295545143244682)
XLA Ops:
  0.0 2.0 %reshape.77 = bf16[8,2,3,8,2,288]{5,4,3,1,2,0:T(2,128)(2,1)S(1)} reshape(bf16[8,2,3,4608]{3,1,2,0:T(2,128)(2,1)} %param.8) | data formatting | bytes 884736 | tf_op jit(solution)/shard_map/reshape | solution.py:152
  2.0 0.4 copy.115
  2.4 0.4 reshape.78
  2.9 8.0 %collective-permute-start.1 = (bf16[4,1,8,896]{3,2,1,0:T(8,128)(2,1)S(1)}, bf16[4,1,8,896]{3,2,1,0:T(8,128)(2,1)S(1)}, u32[]{:S(2)}, u32[]{:S(2)}) collective-permute-start(bf16[4,1,8,896]{3,2,1,0:T(8,128)(2,1)S(1)} %slice_select_fusion), channel_id=1, source_target_pairs={{0,64},{1,65},{2,66},{3,67},{4,452},{5,453},{6,454},{7,455},{64,12... | collective-permute-start | bytes 172040 | tf_op jit(solution)/shard_map/ppermute | solution.py:167
  11.0 2.1 %collective-permute-start = (bf16[4,2,8,896]{3,2,1,0:T(8,128)(2,1)S(1)}, bf16[4,2,8,896]{3,2,1,0:T(8,128)(2,1)S(1)}, u32[]{:S(2)}, u32[]{:S(2)}) collective-permute-start(bf16[4,2,8,896]{3,2,1,0:T(8,128)(2,1)S(1)} %reverse_select_fusion), channel_id=1, source_target_pairs={{0,448},{1,449},{2,450},{3,451},{4,68},{5,69},{6,70},{7,71},{64,0}... | collective-permute-start | bytes 344072 | tf_op jit(solution)/shard_map/ppermute | solution.py:166
  13.1 0.1 pad_maximum_fusion.1
  13.2 5.3 %collective-permute-start.3 = (bf16[3,8,8,896]{3,2,1,0:T(8,128)(2,1)S(1)}, bf16[3,8,8,896]{3,2,1,0:T(8,128)(2,1)S(1)}, u32[]{:S(2)}, u32[]{:S(2)}) collective-permute-start(bf16[3,8,8,896]{3,2,1,0:T(8,128)(2,1)S(1)} %get-tuple-element.19), channel_id=1, source_target_pairs={{0,56},{8,0},{16,8},{24,16},{32,24},{40,32},{48,40},{56,48},{1,57}... | collective-permute-start | bytes 1032200 | tf_op jit(solution)/shard_map/ppermute | solution.py:157
  18.5 1.9 %collective-permute-start.2 = (bf16[3,8,8,896]{3,2,1,0:T(8,128)(2,1)S(1)}, bf16[3,8,8,896]{3,2,1,0:T(8,128)(2,1)S(1)}, u32[]{:S(2)}, u32[]{:S(2)}) collective-permute-start(bf16[3,8,8,896]{3,2,1,0:T(8,128)(2,1)S(1)} %get-tuple-element.20), channel_id=1, source_target_pairs={{0,8},{8,16},{16,24},{24,32},{32,40},{40,48},{48,56},{56,0},{1,9},... | collective-permute-start | bytes 1032200 | tf_op jit(solution)/shard_map/ppermute | solution.py:156
  20.5 0.1 fusion.31
  20.5 0.1 fusion.26
  20.6 0.1 fusion.33
  20.7 0.1 copy.97
  20.8 0.1 copy.96
  21.0 0.1 copy.99
  21.1 0.1 copy.98
  21.3 2.9 %collective-permute-done.3.high_ = bf16[3,8,8,896]{3,2,1,0:T(8,128)(2,1)S(1)} collective-permute-done((bf16[3,8,8,896]{3,2,1,0:T(8,128)(2,1)S(1)}, bf16[3,8,8,896]{3,2,1,0:T(8,128)(2,1)S(1)}, u32[]{:S(2)}, u32[]{:S(2)}) %collective-permute-start.3) | collective-permute-done | bytes 344096 | tf_op jit(solution)/shard_map/ppermute | solution.py:157
  24.2 5.0 %collective-permute-done.2.low = bf16[3,8,8,896]{3,2,1,0:T(8,128)(2,1)S(1)} collective-permute-done((bf16[3,8,8,896]{3,2,1,0:T(8,128)(2,1)S(1)}, bf16[3,8,8,896]{3,2,1,0:T(8,128)(2,1)S(1)}, u32[]{:S(2)}, u32[]{:S(2)}) %collective-permute-start.2) | collective-permute-done | bytes 344096 | tf_op jit(solution)/shard_map/ppermute | solution.py:156
  29.3 2.7 %shard_map.82 = bf16[8,4,8,896]{3,2,1,0:T(8,128)(2,1)} custom-call(s32[1]{0:T(128)} %bitcast.flags, f32[9,2]{1,0:T(8,128)S(1)} %broadcast_select_fusion.face_x, f32[8,3]{1,0:T(8,128)S(1)} %min.7.face_y, bf16[4,8,8,896]{3,2,1,0:T(8,128)(2,1)S(1)} %pad.4.own, bf16[4,2,8,896]{3,2,1,0:T(8,128)(2,1)S(1)} %collective-permute-done.xup, ...), custom_call_target="tpu_custom_call" | custom-call | flops 10000000 | bytes 2000000 | tf_op jit(solution)/shard_map/pallas_call | solution.py:125
  31.9 10.3 %all-to-all-start = ((bf16[8,4,8,896]{3,2,1,0:T(8,128)(2,1)}), bf16[8,4,8,896]{3,2,1,0:T(8,128)(2,1)S(1)}, u32[]{:S(2)}, u32[]{:S(2)}) async-start(bf16[8,4,8,896]{3,2,1,0:T(8,128)(2,1)} %shard_map.82), calls=%async_computation | async-start | bytes 917504 | tf_op jit(solution)/shard_map/all_to_all | solution.py:188
  42.3 0.7 slice_reduce_fusion
  43.0 0.1 mul.133
  43.1 0.1 mul.128
  43.1 0.1 mul.125
  43.2 0.1 mul.120
  43.3 0.1 mul.117
  43.4 0.2 multiply_reduce_fusion
  43.6 0.2 select_reduce_fusion
  43.7 15.1 %all-to-all-done = bf16[8,4,8,896]{3,2,1,0:T(8,128)(2,1)S(1)} async-done(((bf16[8,4,8,896]{3,2,1,0:T(8,128)(2,1)}), bf16[8,4,8,896]{3,2,1,0:T(8,128)(2,1)S(1)}, u32[]{:S(2)}, u32[]{:S(2)}) %all-to-all-start) | async-done | bytes 458784 | tf_op jit(solution)/shard_map/all_to_all | solution.py:188
  58.8 0.5 reshape.79
  59.4 0.5 copy.61
  59.9 0.4 reshape.80
  60.3 0.4 convolution_bitcast_fusion
  60.7 0.5 copy-done.1
  61.3 1.6 %broadcast_multiply_fusion = (f32[2,24,8,576]{3,2,1,0:T(8,128)S(1)}, f32[2,24,8,576]{3,2,1,0:T(8,128)S(1)}, f32[2,24,8,576]{3,2,1,0:T(8,128)S(1)}) fusion(f32[24,576]{1,0:T(8,128)S(1)} %mul.125, f32[24,576]{1,0:T(8,128)S(1)} %mul.117, f32[576,576,1,1]{1,0,3,2:T(8,128)S(1)} %copy-done.1, f32[2,24,8,576]{3,1,2,0:T(8,128)S(1)} %convolution_bitcast_fusion), kind=kOutput, calls=%fused_computation.25 | convolution fusion | flops 764854272 | bytes 4976640 | tf_op jit(solution)/shard_map/nalc,cd->nald/dot_general | solution.py:137
  62.9 0.6 convolution_bitcast_fusion.3
  63.5 1.5 %fusion.37 = f32[2,24,8,576]{3,1,2,0:T(8,128)S(1)} fusion(f32[2,24,8,576]{3,1,2,0:T(8,128)S(1)} %convolution_bitcast_fusion.3, f32[576,576,1,1]{1,0,3,2:T(8,128)S(1)} %copy-done.1), kind=kOutput, calls=%fused_computation.83 | convolution fusion | flops 764411904 | bytes 3096576 | tf_op jit(solution)/shard_map/nalc,cd->nald/dot_general | solution.py:137
  65.0 0.6 convolution_bitcast_fusion.5
  65.6 1.5 %fusion.36 = f32[2,24,8,576]{3,1,2,0:T(8,128)S(1)} fusion(f32[2,24,8,576]{3,1,2,0:T(8,128)S(1)} %convolution_bitcast_fusion.5, f32[576,576,1,1]{1,0,3,2:T(8,128)S(1)} %copy-done.1), kind=kOutput, calls=%fused_computation.82 | convolution fusion | flops 764411904 | bytes 3096576 | tf_op jit(solution)/shard_map/nalc,cd->nald/dot_general | solution.py:137
  67.1 0.7 multiply_bitcast_fusion
  67.8 0.6 convolution_bitcast_fusion.1
  68.4 0.6 convolution_bitcast_fusion.2
  69.0 0.6 convolution_bitcast_fusion.4
  69.6 1.8 %convolution_multiply_fusion.2 = f32[2,24,8,576]{3,1,2,0:T(8,128)S(1)} fusion(f32[2,24,8,576]{3,1,2,0:T(8,128)S(1)} %fusion.36, f32[2,24,8,576]{3,1,2,0:T(8,128)S(1)} %convolution_bitcast_fusion.4, f32[576,576,1,1]{1,0,3,2:T(8,128)S(1)} %copy-done.1), kind=kOutput, calls=%fused_computation.12 | convolution fusion | flops 764633088 | bytes 3981312 | tf_op jit(solution)/shard_map/nalc,cd->nald/dot_general | solution.py:137
  71.4 1.6 %fusion.3 = f32[2,24,8,576]{3,1,2,0:T(8,128)S(1)} fusion(f32[2,24,8,576]{3,1,2,0:T(8,128)S(1)} %convolution_multiply_fusion.2, f32[2,24,8,576]{3,1,2,0:T(8,128)S(1)} %fusion.37, f32[2,24,8,576]{3,1,2,0:T(8,128)S(1)} %convolution_bitcast_fusion.2, f32[576,576,1,1]{1,0,3,2:T(8,128)S(1)} %copy-done.1), kind=kOutput, calls=%fused_computation.11 | convolution fusion | flops 764854272 | bytes 4866048 | tf_op jit(solution)/shard_map/nalc,cd->nald/dot_general | solution.py:137
  73.0 1.6 %fusion.4 = bf16[2,24,8,576]{3,1,2,0:T(8,128)(2,1)S(1)} fusion(f32[2,24,8,576]{3,1,2,0:T(8,128)S(1)} %fusion.3, f32[2,24,8,576]{3,1,2,0:T(8,128)S(1)} %convolution_bitcast_fusion.1, f32[576,576,1,1]{1,0,3,2:T(8,128)S(1)} %copy-done.1, bf16[2,24,8,576]{3,1,2,0:T(8,128)(2,1)S(1)} %reshape.80, f32[2]{0:T(128)S(1)} %multiply_reduce_fusion), kind=kOutput, calls=%fused_computation.13 | convolution fusion | flops 765739008 | bytes 3981320 | tf_op jit(solution)/shard_map/nalc,cd->nald/dot_general | solution.py:137
  74.6 0.5 reshape.87
  75.1 18.5 %all_to_all.23 = bf16[1,2,24,4608]{3,1,0,2:T(2,128)(2,1)S(1)} all-to-all(bf16[1,2,24,4608]{3,1,0,2:T(2,128)(2,1)S(1)} %reshape.87), channel_id=1, replica_groups=mesh['gx'=8,'gy'=8,'vert'=8] {'vert'}, dimensions={2} | all-to-all | bytes 884736 | tf_op jit(solution)/shard_map/all_to_all | solution.py:214
  93.7 0.8 copy.117
  (30 shorter events, 0.4 us)
Async XLA Ops:
  2.9 18.4 %collective-permute-start.1 = (bf16[4,1,8,896]{3,2,1,0:T(8,128)(2,1)S(1)}, bf16[4,1,8,896]{3,2,1,0:T(8,128)(2,1)S(1)}, u32[]{:S(2)}, u32[]{:S(2)}) collective-permute-start(bf16[4,1,8,896]{3,2,1,0:T(8,128)(2,1)S(1)} %slice_select_fusion), channel_id=1, source_target_pairs={{0,64},{1,65},{2,66},{3,67},{4,452},{5,453},{6,454},{7,455},{64,12... | collective-permute-start | bytes 172040 | tf_op jit(solution)/shard_map/ppermute | solution.py:167
  10.9 9.5 %copy-start.4 = (s32[64,16]{0,1:T(8,128)S(1)}, s32[64,16]{0,1:T(8,128)}, u32[]{:S(2)}) copy-start(s32[64,16]{0,1:T(8,128)} %param.9) | copy-start | bytes 12292
  11.0 18.3 %copy-start = (f32[2,8,896]{2,1,0:T(8,128)S(1)}, f32[2,8,896]{2,1,0:T(8,128)}, u32[]{:S(2)}) copy-start(f32[2,8,896]{2,1,0:T(8,128)} %constant.69.clone.speeds_y) | copy-start | bytes 172036
  11.0 10.3 %collective-permute-start = (bf16[4,2,8,896]{3,2,1,0:T(8,128)(2,1)S(1)}, bf16[4,2,8,896]{3,2,1,0:T(8,128)(2,1)S(1)}, u32[]{:S(2)}, u32[]{:S(2)}) collective-permute-start(bf16[4,2,8,896]{3,2,1,0:T(8,128)(2,1)S(1)} %reverse_select_fusion), channel_id=1, source_target_pairs={{0,448},{1,449},{2,450},{3,451},{4,68},{5,69},{6,70},{7,71},{64,0}... | collective-permute-start | bytes 344072 | tf_op jit(solution)/shard_map/ppermute | solution.py:166
  13.2 11.0 %collective-permute-start.3 = (bf16[3,8,8,896]{3,2,1,0:T(8,128)(2,1)S(1)}, bf16[3,8,8,896]{3,2,1,0:T(8,128)(2,1)S(1)}, u32[]{:S(2)}, u32[]{:S(2)}) collective-permute-start(bf16[3,8,8,896]{3,2,1,0:T(8,128)(2,1)S(1)} %get-tuple-element.19), channel_id=1, source_target_pairs={{0,56},{8,0},{16,8},{24,16},{32,24},{40,32},{48,40},{56,48},{1,57}... | collective-permute-start | bytes 1032200 | tf_op jit(solution)/shard_map/ppermute | solution.py:157
  18.5 10.7 %collective-permute-start.2 = (bf16[3,8,8,896]{3,2,1,0:T(8,128)(2,1)S(1)}, bf16[3,8,8,896]{3,2,1,0:T(8,128)(2,1)S(1)}, u32[]{:S(2)}, u32[]{:S(2)}) collective-permute-start(bf16[3,8,8,896]{3,2,1,0:T(8,128)(2,1)S(1)} %get-tuple-element.20), channel_id=1, source_target_pairs={{0,8},{8,16},{16,24},{24,32},{32,40},{40,48},{48,56},{56,0},{1,9},... | collective-permute-start | bytes 1032200 | tf_op jit(solution)/shard_map/ppermute | solution.py:156
  21.3 20.9 %copy-start.3 = (f32[5,13824]{1,0:T(8,128)S(1)}, f32[5,13824]{1,0:T(8,128)}, u32[]{:S(2)}) copy-start(f32[5,13824]{1,0:T(8,128)} %param.12) | copy-start | bytes 829444
  31.9 11.7 %copy-start.5 = (s32[8,8]{1,0:T(8,128)S(1)}, s32[8,8]{1,0:T(8,128)}, u32[]{:S(2)}) copy-start(s32[8,8]{1,0:T(8,128)} %param.10) | copy-start | bytes 772
  31.9 11.7 %copy-start.6 = (f32[8]{0:T(128)S(1)}, f32[8]{0:T(128)}, u32[]{:S(2)}) copy-start(f32[8]{0:T(128)} %param.11) | copy-start | bytes 100
  31.9 26.9 %all-to-all-start = ((bf16[8,4,8,896]{3,2,1,0:T(8,128)(2,1)}), bf16[8,4,8,896]{3,2,1,0:T(8,128)(2,1)S(1)}, u32[]{:S(2)}, u32[]{:S(2)}) async-start(bf16[8,4,8,896]{3,2,1,0:T(8,128)(2,1)} %shard_map.82), calls=%async_computation | async-start | bytes 917504 | tf_op jit(solution)/shard_map/all_to_all | solution.py:188
  59.4 0.9 %copy-start.2 = (f32[24,24,1,1]{1,0,3,2:T(8,128)S(1)}, f32[24,24,1,1]{1,0,3,2:T(8,128)}, u32[]{:S(2)}) copy-start(f32[24,24,1,1]{1,0,3,2:T(8,128)} %constant.75) | copy-start | bytes 6916
  59.9 1.4 %copy-start.1 = (f32[576,576,1,1]{1,0,3,2:T(8,128)S(1)}, f32[576,576,1,1]{1,0,3,2:T(8,128)}, u32[]{:S(2)}) copy-start(f32[576,576,1,1]{1,0,3,2:T(8,128)} %constant.76) | copy-start | bytes 3981316
where the time goes:
time: 94.9 us; the launch traced here: 94.5 us
  starting transfers between devices  27.6 us (29%)
  waiting for transfers between devices  23 us (24%)
  blocking collectives  18.5 us (19%)
  matrix products  13.6 us (14%)
  local copies, waits for them, and re-layouts  7.98 us (8%)
  Pallas kernels  2.65 us (3%)
    all_to_all x1, blocking collectives, body(): lax.all_to_all(updated, 'vert', split_axis=2, concat_axis=0, tiled=True)  18.5 us
    all_to_all x1, waiting for transfers between devices, body(): lax.all_to_all(transported, 'vert', split_axis=0, concat_axis=0, tiled=True)  15.1 us
    all_to_all x1, starting transfers between devices, body(): lax.all_to_all(transported, 'vert', split_axis=0, concat_axis=0, tiled=True)  10.3 us
    dot_general x6, matrix products, transform(): return jnp.einsum('nalc,cd->nald', partial_x, table_yz, precision=high)  9.62 us
    ppermute x1, starting transfers between devices, body(): xdn = lax.ppermute(downstream, ('gx', 'vert'), send_down)  8.04 us
    ppermute x1, starting transfers between devices, body(): lax.ppermute(jnp.stack([own[0], own[2], own[1]]), 'gy', ring(count_y, -1))  5.29 us
    ppermute x1, waiting for transfers between devices, body(): lax.ppermute(jnp.stack([own[1], own[3], own[2]]), 'gy', ring(count_y, 1))  5.05 us
    dot_general x6, matrix products, transform(): partial_x = jnp.einsum('ab,nblc->nalc', table_x, fields, precision=high)  3.3 us
  transfers between devices with their start and end apart: 5, of which 3 were waited for; matrix products, arithmetic and copies ran while one was open for 3% of the time, Pallas kernels for 0%

commit v1 on v0

--- a/solution.py
+++ b/solution.py
@@ -1,5 +1,6 @@
 import math
 
+import ml_dtypes
 import numpy as np
 import jax
 import jax.numpy as jnp
@@ -17,10 +18,12 @@
 SUB = 3
 LANES = SUB * HALF
 WIDE = 896
+YZ = 640
+MAIN = 512
+DEPTH = 3 * MAIN + 256
 
 courant = 0.45
 collide_step = 0.4
-high = lax.Precision.HIGH
 
 
 def open_share(wall_mask):
@@ -127,14 +130,228 @@
         out_shape=jax.ShapeDtypeStruct((rows_x, 4, LEVELS, WIDE), jnp.bfloat16),
         in_specs=[smem] * 3 + [vmem] * 7,
         out_specs=vmem,
-        compiler_params=pltpu.CompilerParams(vmem_limit_bytes=32 * 1024 * 1024),
+        compiler_params=pltpu.CompilerParams(vmem_limit_bytes=16 * 1024 * 1024),
         cost_estimate=pl.CostEstimate(flops=10_000_000, bytes_accessed=2_000_000, transcendentals=0),
     )(flag, face_x, face_y, own, xup, xdn, low, high_, speeds_x, speeds_y)
 
 
-def transform(fields, table_x, table_yz):
-    partial_x = jnp.einsum("ab,nblc->nalc", table_x, fields, precision=high)
-    return jnp.einsum("nalc,cd->nald", partial_x, table_yz, precision=high)
+def small(matrix, inputs):
+    products = {}
+
+    def product(scale, n):
+        if scale == 1.0:
+            return inputs[n]
+        if (scale, n) not in products:
+            products[scale, n] = inputs[n] * scale
+        return products[scale, n]
+
+    results = []
+    for row in matrix:
+        total = None
+        for n, value in enumerate(row):
+            value = round(float(value), 12)
+            if value == 0.0:
+                continue
+            term = product(abs(value), n)
+            if total is None:
+                total = term if value > 0 else -term
+            else:
+                total = total + term if value > 0 else total - term
+        results.append(total)
+    return results
+
+
+def trig(function, outs, ins, over):
+    return [[function(math.pi * k * n / over) for n in ins] for k in outs]
+
+
+def cosines(v):
+    e = [v[n] + v[12 - n] for n in range(6)] + [v[6]]
+    o = [v[n] - v[12 - n] for n in range(6)]
+    ee = [e[n] + e[6 - n] for n in range(3)] + [e[3]]
+    eo = [e[n] - e[6 - n] for n in range(3)]
+    out = [None] * 13
+    out[0::4] = small(trig(math.cos, range(4), range(4), 3), ee)
+    out[2::4] = small(trig(math.cos, (1, 3, 5), range(3), 6), eo)
+    out[1::2] = small(trig(math.cos, (1, 3, 5, 7, 9, 11), range(6), 12), o)
+    return out
+
+
+def sines(v):
+    v = [None] + v
+    f = [v[n] + v[12 - n] for n in range(1, 6)] + [v[6]]
+    g = [None] + [v[n] - v[12 - n] for n in range(1, 6)]
+    gp = [g[1] + g[5], g[2] + g[4], g[3]]
+    gm = [g[1] - g[5], g[2] - g[4]]
+    out = [None] * 11
+    out[0::2] = small(trig(math.sin, (1, 3, 5, 7, 9, 11), range(1, 7), 12), f)
+    out[1::4] = small(trig(math.sin, (1, 3, 5), (1, 2, 3), 6), gp)
+    out[3::4] = small(trig(math.sin, (2, 4), (1, 2), 6), gm)
+    return out
+
+
+def modes_of(x):
+    even = [x[0]] + [x[n] + x[VX - n] for n in range(1, 12)] + [x[12]]
+    odd = [x[n] - x[VX - n] for n in range(1, 12)]
+    return cosines(even) + sines(odd)
+
+
+def points_of(modes):
+    p = cosines(modes[:13])
+    q = sines(modes[13:])
+    out = [None] * VX
+    out[0], out[12] = p[0], p[12]
+    for n in range(1, 12):
+        out[n] = p[n] + q[n - 1]
+        out[VX - n] = p[n] - q[n - 1]
+    return out
+
+
+def split_table():
+    table = np.kron(cas_matrix(VY), cas_matrix(VZ)).astype(np.float32)
+    table = np.pad(table, ((0, 0), (0, YZ - PLANE)))
+    top = table.astype(ml_dtypes.bfloat16)
+    low = (table - top.astype(np.float32)).astype(ml_dtypes.bfloat16)
+    rest = PLANE - MAIN
+    back = np.zeros((DEPTH, YZ), ml_dtypes.bfloat16)
+    back[0:MAIN] = top[:MAIN]
+    back[MAIN : 2 * MAIN] = top[:MAIN]
+    back[2 * MAIN : 3 * MAIN] = low[:MAIN]
+    back[3 * MAIN : 3 * MAIN + rest] = top[MAIN:PLANE]
+    back[3 * MAIN + rest : 3 * MAIN + 2 * rest] = top[MAIN:PLANE]
+    back[3 * MAIN + 128 : 3 * MAIN + 128 + rest] = low[MAIN:PLANE]
+    return back
+
+
+def collide_kernel(
+    weights, block, bank, coefs, back, out, g, spec, mixed, lhs, left, gain
+):
+    cells = block.shape[1] // 2
+    per_cell = VX * LEVELS
+    blank = jnp.zeros((LEVELS, YZ - PLANE), jnp.float32)
+
+    def plane(cell, a):
+        source, i = a // SUB, a % SUB
+        wide = [block[source, 2 * cell + half].astype(jnp.float32) for half in range(2)]
+        cut = [part[:, i * HALF : (i + 1) * HALF] for part in wide]
+        return jnp.concatenate(cut + [blank], axis=1)
+
+    for cell in range(cells):
+        for m in range(VX // 2):
+            pair = jnp.concatenate([plane(cell, 2 * m), plane(cell, 2 * m + 1)], axis=0)
+            at_rows = pl.ds(cell * per_cell + 2 * m * LEVELS, 2 * LEVELS)
+            g[at_rows, :] = pair.astype(jnp.bfloat16)
+
+    tiles = YZ // 128
+    chunks = ((0, 256), (256, 256), (512, 128))
+
+    edge = jnp.concatenate([g[:, MAIN:], g[:, MAIN:]], axis=1)
+    for start, width in chunks:
+        cols = pl.ds(start, width)
+        total = jnp.dot(edge, back[3 * MAIN :, cols], preferred_element_type=jnp.float32)
+        for first in (0, 2 * MAIN):
+            total = total + jnp.dot(
+                g[:, :MAIN], back[pl.ds(first, MAIN), cols], preferred_element_type=jnp.float32
+            )
+        spec[:, cols] = total
+
+    def rows(base, a, count=LEVELS):
+        return pl.ds(base + a * LEVELS, count)
+
+    def ahead(index):
+        base, lanes = index // tiles * per_cell, pl.ds(index % tiles * 128, 128)
+        modes = modes_of([spec[rows(base, a), lanes] for a in range(VX)])
+        for a in range(VX):
+            total = coefs[0] * modes[a]
+            for shift in range(1, LEVELS):
+                total = total + coefs[shift] * pltpu.roll(modes[a], shift, 0)
+            spec[rows(base, a), lanes] = modes[a]
+            mixed[rows(base, a), lanes] = total
+
+    for index in range(cells * tiles):
+        ahead(index)
+
+    lane = lax.broadcasted_iota(jnp.int32, (2 * LEVELS, 128), 1)
+
+    def prepare(slot, which, source, base, lanes, t, last):
+        factors = [bank[which, pl.ds(k, 1), lanes] for k in range(13)]
+        points = points_of(
+            [source[rows(base, a), lanes] * factors[a if a < 13 else a - 12] for a in range(VX)]
+        )
+        for m in range(VX // 2):
+            pair = jnp.concatenate([points[2 * m], points[2 * m + 1]], axis=0)
+            top = pair.astype(jnp.bfloat16)
+            rest = pair - top.astype(jnp.float32)
+            at_rows = rows(base, 2 * m, 2 * LEVELS)
+
+            def put(start, value):
+                lhs[slot, at_rows, pl.ds(start, 128)] = value
+
+            if last:
+                both = jnp.where(lane < PLANE - MAIN, pair, pltpu.roll(rest, 64, 1))
+                put(3 * MAIN, both.astype(jnp.bfloat16))
+                put(3 * MAIN + 128, top)
+            else:
+                put(t * 128, top)
+                put(MAIN + t * 128, rest.astype(jnp.bfloat16))
+                put(2 * MAIN + t * 128, top)
+
+    def prepare_all(slot, which, source):
+        for cell in range(cells):
+            for t in range(tiles):
+                base = cell * per_cell
+                prepare(slot, which, source, base, pl.ds(t * 128, 128), t, t == tiles - 1)
+
+    def product(slot, start, width):
+        return jnp.dot(
+            lhs[slot], back[:, pl.ds(start, width)], preferred_element_type=jnp.float32
+        )
+
+    for direction in range(2):
+        prepare_all(0, direction, spec)
+        prepare_all(1, 2 + direction, mixed)
+        for start, width in chunks:
+            left[:, pl.ds(start, width)] = product(0, start, width)
+        for start, width in chunks:
+            cols = pl.ds(start, width)
+            value = left[:, cols] * product(1, start, width)
+            gain[:, cols] = value if direction == 0 else gain[:, cols] + value
+    prepare_all(0, 4, mixed)
+    for start, width in chunks:
+        loss = product(0, start, width)
+        for cell in range(cells):
+            at_rows = pl.ds(cell * per_cell, per_cell)
+            keep = min(width, PLANE - start)
+            fields = g[at_rows, pl.ds(start, width)].astype(jnp.float32)
+            part = loss[cell * per_cell : (cell + 1) * per_cell]
+            value = fields + weights[cell] * (
+                gain[at_rows, pl.ds(start, width)] - fields * part
+            )
+            out[at_rows, pl.ds(start, keep)] = value[:, :keep].astype(jnp.bfloat16)
+
+
+def collide(weights, block, bank, coefs, back):
+    count = block.shape[1] // 2 * VX * LEVELS
+    smem = pl.BlockSpec(memory_space=pltpu.SMEM)
+    vmem = pl.BlockSpec(memory_space=pltpu.VMEM)
+    return pl.pallas_call(
+        collide_kernel,
+        out_shape=jax.ShapeDtypeStruct((count, PLANE), jnp.bfloat16),
+        in_specs=[smem] + [vmem] * 4,
+        out_specs=vmem,
+        scratch_shapes=[
+            pltpu.VMEM((count, YZ), jnp.bfloat16),
+            pltpu.VMEM((count, YZ), jnp.float32),
+            pltpu.VMEM((count, YZ), jnp.float32),
+            pltpu.VMEM((2, count, DEPTH), jnp.bfloat16),
+            pltpu.VMEM((count, YZ), jnp.float32),
+            pltpu.VMEM((count, YZ), jnp.float32),
+        ],
+        compiler_params=pltpu.CompilerParams(vmem_limit_bytes=16 * 1024 * 1024),
+        cost_estimate=pl.CostEstimate(
+            flops=8_000_000_000, bytes_accessed=8_000_000, transcendentals=0
+        ),
+    )(weights, block, bank, coefs, back)
 
 
 def ring(count, step):
@@ -155,17 +372,6 @@
 
     low = lax.ppermute(jnp.stack([own[1], own[3], own[2]]), "gy", ring(count_y, 1))
     high_ = lax.ppermute(jnp.stack([own[0], own[2], own[1]]), "gy", ring(count_y, -1))
-    upstream = jnp.where(forward, own[:, rows_x - 2 :], own[:, 1::-1])
-    downstream = jnp.where(forward, own[:, :1], own[:, rows_x - 1 :])
-    send_up, send_down = [], []
-    for i in range(count_x):
-        for v in range(count_v):
-            step = 1 if v >= count_v // 2 else -1
-            send_up.append((i * count_v + v, (i + step) % count_x * count_v + v))
-            send_down.append((i * count_v + v, (i - step) % count_x * count_v + v))
-    xup = lax.ppermute(upstream, ("gx", "vert"), send_up)
-    xdn = lax.ppermute(downstream, ("gx", "vert"), send_down)
-
     openness = open_share(wall_mask)
     wrapped = jnp.pad(openness, 1, mode="wrap")
     anchor_x = lax.axis_index("gx") * rows_x
@@ -176,6 +382,18 @@
     face_x = jnp.where(forward, face_x, face_x[::-1])
     open_y = window[1 : rows_x + 1]
     face_y = jnp.minimum(open_y[:, :-1], open_y[:, 1:])
+    own_x, face_x, face_y = lax.optimization_barrier((own, face_x, face_y))
+    upstream = jnp.where(forward, own_x[:, rows_x - 2 :], own_x[:, 1::-1])
+    downstream = jnp.where(forward, own_x[:, :1], own_x[:, rows_x - 1 :])
+    send_up, send_down = [], []
+    for i in range(count_x):
+        for v in range(count_v):
+            step = 1 if v >= count_v // 2 else -1
+            send_up.append((i * count_v + v, (i + step) % count_x * count_v + v))
+            send_down.append((i * count_v + v, (i - step) % count_x * count_v + v))
+    xup = lax.ppermute(upstream, ("gx", "vert"), send_up)
+    xdn = lax.ppermute(downstream, ("gx", "vert"), send_down)
+
     own_open = lax.dynamic_slice(openness, (anchor_x + at_v, anchor_y), (1, rows_y))[0]
 
     index_x = at_v * local_vx + jnp.arange(WIDE, dtype=jnp.int32) // HALF
@@ -186,9 +404,6 @@
     transported = transport(flag, face_x, face_y, own, xup, xdn, low, high_, speeds_x, speeds_y)
 
     block = lax.all_to_all(transported, "vert", split_axis=0, concat_axis=0, tiled=True)
-    fields = block[..., :LANES].reshape(count_v, 2, 2, LEVELS, SUB, HALF)
-    fields = fields.transpose(1, 0, 4, 3, 2, 5).reshape(2, VX, LEVELS, PLANE).astype(jnp.float32)
-
     entries = jnp.arange(trans_weight.shape[0], dtype=jnp.int32)
     mixing = jnp.sum(
         jnp.where(
@@ -196,20 +411,18 @@
         ),
         axis=-1,
     )
-    table_x = jnp.asarray(cas_matrix(VX).astype(np.float32))
-    table_yz = jnp.asarray(np.kron(cas_matrix(VY), cas_matrix(VZ)).astype(np.float32))
-    bank = kernels.reshape(kernels.shape[0], VX, 1, PLANE) / float(VX * PLANE)
-    spectrum = transform(fields, table_x, table_yz)
-    mixed_spectrum = jnp.einsum("lm,namc->nalc", mixing, spectrum, precision=high)
-    gain_term = jnp.zeros_like(fields)
-    for direction in range(2):
-        gain_left = transform(bank[direction] * spectrum, table_x, table_yz)
-        gain_right = transform(bank[2 + direction] * mixed_spectrum, table_x, table_yz)
-        gain_term = gain_term + gain_left * gain_right
-    loss_term = transform(bank[4] * mixed_spectrum, table_x, table_yz)
-    collision = gain_term - fields * loss_term
-    weights = own_open.reshape(2, 1, 1, 1)
-    updated = (fields + collide_step * weights * collision).astype(jnp.bfloat16)
+    level = np.arange(LEVELS)
+    chosen = (level[None, :, None] - level[:, None, None]) % LEVELS == level[None, None, :]
+    coefs = jnp.sum(jnp.where(chosen, mixing[None], 0.0), axis=-1)
+    coefs = jnp.broadcast_to(coefs[:, :, None], (LEVELS, LEVELS, 128))
+    bank = kernels.reshape(kernels.shape[0], VX, PLANE)[:, : VX // 2 + 1]
+    twice = np.full((VX // 2 + 1,), 2.0, np.float32)
+    twice[0] = twice[VX // 2] = 1.0
+    bank = bank * (twice / float(VX * PLANE)).reshape(1, -1, 1)
+    bank = jnp.pad(bank, ((0, 0), (0, 0), (0, YZ - PLANE)))
+    updated = collide(
+        collide_step * own_open, block, bank, coefs, jnp.asarray(split_table())
+    )
     updated = updated.reshape(1, 2, VX, row_width)
     return lax.all_to_all(updated, "vert", split_axis=2, concat_axis=0, tiled=True)
 

time: 94.9 us -> 83.3 us (0.88); the launches traced: 94.5 us -> 81.7 us
  matrix products: 13.6 us -> 0 us
  Pallas kernels: 2.65 us -> 12.2 us
  waiting for transfers between devices: 23 us -> 15.5 us
  local copies, waits for them, and re-layouts: 7.98 us -> 6.22 us
    dot_general x13 -> x0, matrix products: 13.6 us -> none  [the longest x6 9.62 us: transform(): return jnp.einsum('nalc,cd->nald', partial_x, table_yz, precision=high)]
    pallas_call x0 -> x1, Pallas kernels: none -> 9.54 us  [collide(): pl.pallas_call(collide_kernel, out_shape=jax.ShapeDtypeStruct((count, PLA...]
    ppermute x1, waiting for transfers between devices: 5.05 us -> 0.01 us  [body(): lax.ppermute(jnp.stack([own[1], own[3], own[2]]), 'gy', ring(count_y, 1))]
    ppermute x1, starting transfers between devices: 8.04 us -> 3.91 us  [body(): xdn = lax.ppermute(downstream, ('gx', 'vert'), send_down)]
    ppermute x1, starting transfers between devices: 5.29 us -> 8.59 us  [body(): lax.ppermute(jnp.stack([own[0], own[2], own[1]]), 'gy', ring(count_y, -1))]
    ppermute x1, waiting for transfers between devices: 2.88 us -> 0.01 us  [body(): lax.ppermute(jnp.stack([own[0], own[2], own[1]]), 'gy', ring(count_y, -1))]
    ppermute x1, starting transfers between devices: 1.92 us -> 4 us  [body(): lax.ppermute(jnp.stack([own[1], own[3], own[2]]), 'gy', ring(count_y, 1))]
    all_to_all x1, starting transfers between devices: 10.3 us -> 8.59 us  [body(): lax.all_to_all(transported, 'vert', split_axis=0, concat_axis=0, tiled=True)]
  transfers between devices with their start and end apart: 5 -> 5, of which waited for: 3 -> 2; matrix products, arithmetic and copies ran while one was open for 3% -> 3% of each run, Pallas kernels for 0% -> 0%
where the time goes in v1:
time: 83.3 us; the launch traced here: 81.7 us
  starting transfers between devices  28.1 us (34%)
  blocking collectives  18.6 us (22%)
  waiting for transfers between devices  15.5 us (19%)
  Pallas kernels  12.2 us (15%)
  local copies, waits for them, and re-layouts  6.22 us (7%)
    all_to_all x1, blocking collectives, body(): lax.all_to_all(updated, 'vert', split_axis=2, concat_axis=0, tiled=True)  18.6 us
    all_to_all x1, waiting for transfers between devices, body(): lax.all_to_all(transported, 'vert', split_axis=0, concat_axis=0, tiled=True)  14.3 us
    pallas_call x1, Pallas kernels, collide(): pl.pallas_call(collide_kernel, out_shape=jax.ShapeDtypeStruct((count, PLA...  9.54 us
    all_to_all x1, starting transfers between devices, body(): lax.all_to_all(transported, 'vert', split_axis=0, concat_axis=0, tiled=True)  8.59 us
    ppermute x1, starting transfers between devices, body(): lax.ppermute(jnp.stack([own[0], own[2], own[1]]), 'gy', ring(count_y, -1))  8.59 us
    ppermute x1, starting transfers between devices, body(): lax.ppermute(jnp.stack([own[1], own[3], own[2]]), 'gy', ring(count_y, 1))  4 us
    ppermute x1, starting transfers between devices, body(): xdn = lax.ppermute(downstream, ('gx', 'vert'), send_down)  3.91 us
    ppermute x1, starting transfers between devices, body(): xup = lax.ppermute(upstream, ('gx', 'vert'), send_up)  3 us
  transfers between devices with their start and end apart: 5, of which 2 were waited for; matrix products, arithmetic and copies ran while one was open for 3% of the time, Pallas kernels for 0%

profile of v1, /device:TPU:7, one launch (start us, length us, event | category | flops | bytes accessed | tf_op | source)
XLA Modules:
  0.0 81.7 jit_solution(6509296450195725205)
XLA Ops:
  0.0 2.0 %reshape.44 = bf16[8,2,3,8,2,288]{5,4,3,1,2,0:T(2,128)(2,1)S(1)} reshape(bf16[8,2,3,4608]{3,1,2,0:T(2,128)(2,1)} %param.9) | data formatting | bytes 884736 | tf_op jit(solution)/shard_map/reshape | solution.py:369
  2.0 0.0 copy-start.2
  2.0 0.4 copy.37
  2.4 0.4 reshape.45
  2.9 0.0 copy-start
  2.9 0.1 pad_maximum_fusion.1
  3.0 4.0 %collective-permute-start.2 = (bf16[3,8,8,896]{3,2,1,0:T(8,128)(2,1)S(1)}, bf16[3,8,8,896]{3,2,1,0:T(8,128)(2,1)S(1)}, u32[]{:S(2)}, u32[]{:S(2)}) collective-permute-start(bf16[3,8,8,896]{3,2,1,0:T(8,128)(2,1)S(1)} %get-tuple-element.16), channel_id=1, source_target_pairs={{0,8},{8,16},{16,24},{24,32},{32,40},{40,48},{48,56},{56,0},{1,9},... | collective-permute-start | bytes 1032200 | tf_op jit(solution)/shard_map/ppermute | solution.py:373
  7.0 8.6 %collective-permute-start.3 = (bf16[3,8,8,896]{3,2,1,0:T(8,128)(2,1)S(1)}, bf16[3,8,8,896]{3,2,1,0:T(8,128)(2,1)S(1)}, u32[]{:S(2)}, u32[]{:S(2)}) collective-permute-start(bf16[3,8,8,896]{3,2,1,0:T(8,128)(2,1)S(1)} %get-tuple-element.15), channel_id=1, source_target_pairs={{0,56},{8,0},{16,8},{24,16},{32,24},{40,32},{48,40},{56,48},{1,57}... | collective-permute-start | bytes 1032200 | tf_op jit(solution)/shard_map/ppermute | solution.py:374
  15.6 0.0 copy-done.2
  15.7 0.1 fusion.17
  15.7 0.1 fusion.12
  15.8 0.1 fusion.19
  15.9 0.1 fusion.18
  16.0 0.1 pad.8.own
  16.0 0.0 copy-start.5
  16.1 0.1 copy.32
  16.1 0.1 copy.33
  16.3 0.1 copy.34
  16.3 0.1 copy.35
  16.5 0.0 copy-start.4
  16.5 0.0 copy-start.6
  16.5 0.0 copy-start.3
  16.5 3.0 %collective-permute-start = (bf16[4,2,8,896]{3,2,1,0:T(8,128)(2,1)S(1)}, bf16[4,2,8,896]{3,2,1,0:T(8,128)(2,1)S(1)}, u32[]{:S(2)}, u32[]{:S(2)}) collective-permute-start(bf16[4,2,8,896]{3,2,1,0:T(8,128)(2,1)S(1)} %reverse_select_fusion), channel_id=1, source_target_pairs={{0,448},{1,449},{2,450},{3,451},{4,68},{5,69},{6,70},{7,71},{64,0}... | collective-permute-start | bytes 344072 | tf_op jit(solution)/shard_map/ppermute | solution.py:394
  19.6 3.9 %collective-permute-start.1 = (bf16[4,1,8,896]{3,2,1,0:T(8,128)(2,1)S(1)}, bf16[4,1,8,896]{3,2,1,0:T(8,128)(2,1)S(1)}, u32[]{:S(2)}, u32[]{:S(2)}) collective-permute-start(bf16[4,1,8,896]{3,2,1,0:T(8,128)(2,1)S(1)} %slice_select_fusion), channel_id=1, source_target_pairs={{0,64},{1,65},{2,66},{3,67},{4,452},{5,453},{6,454},{7,455},{64,12... | collective-permute-start | bytes 172040 | tf_op jit(solution)/shard_map/ppermute | solution.py:395
  23.5 1.2 %collective-permute-done.1.xdn = bf16[4,1,8,896]{3,2,1,0:T(8,128)(2,1)S(1)} collective-permute-done((bf16[4,1,8,896]{3,2,1,0:T(8,128)(2,1)S(1)}, bf16[4,1,8,896]{3,2,1,0:T(8,128)(2,1)S(1)}, u32[]{:S(2)}, u32[]{:S(2)}) %collective-permute-start.1) | collective-permute-done | bytes 57376 | tf_op jit(solution)/shard_map/ppermute | solution.py:395
  24.7 0.0 collective-permute-done.xup
  24.7 0.0 collective-permute-done.2.low
  24.7 0.0 collective-permute-done.3.high_
  24.7 0.0 copy-done
  24.7 2.7 %shard_map.91 = bf16[8,4,8,896]{3,2,1,0:T(8,128)(2,1)} custom-call(s32[1]{0:T(128)} %bitcast.flags, f32[9,2]{1,0:T(8,128)S(1)} %broadcast_select_fusion.face_x, f32[8,3]{1,0:T(8,128)S(1)} %min.7.face_y, bf16[4,8,8,896]{3,2,1,0:T(8,128)(2,1)S(1)} %pad.8.own, bf16[4,2,8,896]{3,2,1,0:T(8,128)(2,1)S(1)} %collective-permute-done.xup, ...), custom_call_target="tpu_custom_call" | custom-call | flops 10000000 | bytes 2000000 | tf_op jit(solution)/shard_map/pallas_call | solution.py:128
  27.4 8.6 %all-to-all-start = ((bf16[8,4,8,896]{3,2,1,0:T(8,128)(2,1)}), bf16[8,4,8,896]{3,2,1,0:T(8,128)(2,1)S(1)}, u32[]{:S(2)}, u32[]{:S(2)}) async-start(bf16[8,4,8,896]{3,2,1,0:T(8,128)(2,1)} %shard_map.91), calls=%async_computation | async-start | bytes 917504 | tf_op jit(solution)/shard_map/all_to_all | solution.py:406
  36.0 1.1 %reshape.46 = f32[5,24,576]{2,1,0:T(8,128)S(1)} reshape(f32[5,13824]{1,0:T(8,128)} %param.13) | data formatting | bytes 552960 | tf_op jit(solution)/shard_map/reshape | solution.py:418
  37.1 0.0 copy-done.5
  37.1 0.1 slice_multiply_fusion
  37.2 0.2 multiply_reduce_fusion.weights
  37.4 0.0 copy-done.4
  37.4 0.0 copy-done.6
  37.5 0.2 select_reduce_fusion.1
  37.6 0.0 copy-done.3
  37.6 0.1 select_reduce_fusion
  37.7 14.3 %all-to-all-done.block = bf16[8,4,8,896]{3,2,1,0:T(8,128)(2,1)S(1)} async-done(((bf16[8,4,8,896]{3,2,1,0:T(8,128)(2,1)}), bf16[8,4,8,896]{3,2,1,0:T(8,128)(2,1)S(1)}, u32[]{:S(2)}, u32[]{:S(2)}) %all-to-all-start) | async-done | bytes 458784 | tf_op jit(solution)/shard_map/all_to_all | solution.py:406
  52.0 0.1 broadcast_in_dim.57.coefs
  52.1 0.0 copy-done.1
  52.1 9.5 %shard_map.92 = bf16[384,576]{1,0:T(8,128)(2,1)S(1)} custom-call(f32[2]{0:T(128)S(1)} %multiply_reduce_fusion.weights, bf16[8,4,8,896]{3,2,1,0:T(8,128)(2,1)S(1)} %all-to-all-done.block, f32[5,13,640]{2,1,0:T(8,128)S(1)} %pad.9.bank, f32[8,8,128]{2,1,0:T(8,128)S(1)} %broadcast_in_dim.57.coefs, bf16[1792,640]{1,0:T(8,128)(2,1)S(1)} %copy-done.1), custom_call_target="tpu_custom_call" | custom-call | flops 8000000000 | bytes 8000000 | tf_op jit(solution)/shard_map/pallas_call | solution.py:337
  61.6 0.3 reshape.47
  62.0 0.3 copy.30
  62.3 18.6 %all_to_all.23 = bf16[1,2,24,4608]{3,1,0,2:T(2,128)(2,1)S(1)} all-to-all(bf16[1,2,24,4608]{3,1,0,2:T(2,128)(2,1)S(1)} %copy.30), channel_id=1, replica_groups=mesh['gx'=8,'gy'=8,'vert'=8] {'vert'}, dimensions={2} | all-to-all | bytes 884736 | tf_op jit(solution)/shard_map/all_to_all | solution.py:427
  80.9 0.8 copy.39
  (13 shorter events, 0.2 us)
Async XLA Ops:
  2.0 13.6 %copy-start.2 = (s32[64,16]{0,1:T(8,128)S(1)}, s32[64,16]{0,1:T(8,128)}, u32[]{:S(2)}) copy-start(s32[64,16]{0,1:T(8,128)} %param.10) | copy-start | bytes 12292
  2.9 21.9 %copy-start = (f32[2,8,896]{2,1,0:T(8,128)S(1)}, f32[2,8,896]{2,1,0:T(8,128)}, u32[]{:S(2)}) copy-start(f32[2,8,896]{2,1,0:T(8,128)} %constant.69.clone.speeds_y) | copy-start | bytes 172036
  3.0 21.7 %collective-permute-start.2 = (bf16[3,8,8,896]{3,2,1,0:T(8,128)(2,1)S(1)}, bf16[3,8,8,896]{3,2,1,0:T(8,128)(2,1)S(1)}, u32[]{:S(2)}, u32[]{:S(2)}) collective-permute-start(bf16[3,8,8,896]{3,2,1,0:T(8,128)(2,1)S(1)} %get-tuple-element.16), channel_id=1, source_target_pairs={{0,8},{8,16},{16,24},{24,32},{32,40},{40,48},{48,56},{56,0},{1,9},... | collective-permute-start | bytes 1032200 | tf_op jit(solution)/shard_map/ppermute | solution.py:373
  7.0 17.7 %collective-permute-start.3 = (bf16[3,8,8,896]{3,2,1,0:T(8,128)(2,1)S(1)}, bf16[3,8,8,896]{3,2,1,0:T(8,128)(2,1)S(1)}, u32[]{:S(2)}, u32[]{:S(2)}) collective-permute-start(bf16[3,8,8,896]{3,2,1,0:T(8,128)(2,1)S(1)} %get-tuple-element.15), channel_id=1, source_target_pairs={{0,56},{8,0},{16,8},{24,16},{32,24},{40,32},{48,40},{56,48},{1,57}... | collective-permute-start | bytes 1032200 | tf_op jit(solution)/shard_map/ppermute | solution.py:374
  16.0 21.1 %copy-start.5 = (f32[13]{0:T(128)S(1)}, f32[13]{0:T(128)}, u32[]{:S(2)}) copy-start(f32[13]{0:T(128)} %constant.78) | copy-start | bytes 160
  16.5 21.0 %copy-start.4 = (s32[8,8]{1,0:T(8,128)S(1)}, s32[8,8]{1,0:T(8,128)}, u32[]{:S(2)}) copy-start(s32[8,8]{1,0:T(8,128)} %param.11) | copy-start | bytes 772
  16.5 20.9 %copy-start.6 = (f32[8]{0:T(128)S(1)}, f32[8]{0:T(128)}, u32[]{:S(2)}) copy-start(f32[8]{0:T(128)} %param.12) | copy-start | bytes 100
  16.5 21.1 %copy-start.3 = (pred[8,8,8]{2,1,0:T(8,128)(4,1)S(1)}, pred[8,8,8]{2,1,0:T(8,128)(4,1)}, u32[]{:S(2)}) copy-start(pred[8,8,8]{2,1,0:T(8,128)(4,1)} %constant.70.clone) | copy-start | bytes 1540
  16.5 8.2 %collective-permute-start = (bf16[4,2,8,896]{3,2,1,0:T(8,128)(2,1)S(1)}, bf16[4,2,8,896]{3,2,1,0:T(8,128)(2,1)S(1)}, u32[]{:S(2)}, u32[]{:S(2)}) collective-permute-start(bf16[4,2,8,896]{3,2,1,0:T(8,128)(2,1)S(1)} %reverse_select_fusion), channel_id=1, source_target_pairs={{0,448},{1,449},{2,450},{3,451},{4,68},{5,69},{6,70},{7,71},{64,0}... | collective-permute-start | bytes 344072 | tf_op jit(solution)/shard_map/ppermute | solution.py:394
  19.6 5.2 %collective-permute-start.1 = (bf16[4,1,8,896]{3,2,1,0:T(8,128)(2,1)S(1)}, bf16[4,1,8,896]{3,2,1,0:T(8,128)(2,1)S(1)}, u32[]{:S(2)}, u32[]{:S(2)}) collective-permute-start(bf16[4,1,8,896]{3,2,1,0:T(8,128)(2,1)S(1)} %slice_select_fusion), channel_id=1, source_target_pairs={{0,64},{1,65},{2,66},{3,67},{4,452},{5,453},{6,454},{7,455},{64,12... | collective-permute-start | bytes 172040 | tf_op jit(solution)/shard_map/ppermute | solution.py:395
  27.4 24.7 %copy-start.1 = (bf16[1792,640]{1,0:T(8,128)(2,1)S(1)}, bf16[1792,640]{1,0:T(8,128)(2,1)}, u32[]{:S(2)}) copy-start(bf16[1792,640]{1,0:T(8,128)(2,1)} %constant.72.clone.back) | copy-start | bytes 6881284
  27.4 24.6 %all-to-all-start = ((bf16[8,4,8,896]{3,2,1,0:T(8,128)(2,1)}), bf16[8,4,8,896]{3,2,1,0:T(8,128)(2,1)S(1)}, u32[]{:S(2)}, u32[]{:S(2)}) async-start(bf16[8,4,8,896]{3,2,1,0:T(8,128)(2,1)} %shard_map.91), calls=%async_computation | async-start | bytes 917504 | tf_op jit(solution)/shard_map/all_to_all | solution.py:406

commit v2 on v1

--- a/solution.py
+++ b/solution.py
@@ -21,6 +21,8 @@
 YZ = 640
 MAIN = 512
 DEPTH = 3 * MAIN + 256
+HIGH_ORDER = (1, 3, 2)
+LOW_ORDER = (0, 2, 1)
 
 courant = 0.45
 collide_step = 0.4
@@ -54,7 +56,45 @@
     return jnp.maximum(jnp.minimum(a, b), jnp.minimum(jnp.maximum(a, b), 0.0))
 
 
-def transport_kernel(flags, face_x, face_y, own, xup, xdn, low, high_, speeds_x, speeds_y, out):
+def split_kernel(flags, raw, own, to_low, to_high, to_down, to_up):
+    rows_x = raw.shape[0]
+    blank = jnp.zeros((LEVELS, WIDE - LANES), jnp.float32)
+    for x in range(rows_x):
+        for y in range(2):
+            wide = [raw[x, i, y].astype(jnp.float32) for i in range(SUB)]
+            for half in range(2):
+                q = 2 * y + half
+                cut = [part[:, half * HALF : (half + 1) * HALF] for part in wide]
+                value = jnp.concatenate(cut + [blank], axis=1).astype(jnp.bfloat16)
+                own[q, x] = value
+                if q in HIGH_ORDER:
+                    to_high[HIGH_ORDER.index(q), x] = value
+                if q in LOW_ORDER:
+                    to_low[LOW_ORDER.index(q), x] = value
+    forward = flags[0] > 0
+    for q in range(4):
+        for step in range(2):
+            row = jnp.where(forward, rows_x - 2 + step, 1 - step)
+            to_down[q, step] = own[q, row]
+        to_up[q, 0] = own[q, jnp.where(forward, 0, rows_x - 1)]
+
+
+def split(flag, raw):
+    rows_x = raw.shape[0]
+    smem = pl.BlockSpec(memory_space=pltpu.SMEM)
+    vmem = pl.BlockSpec(memory_space=pltpu.VMEM)
+    shapes = [(4, rows_x), (3, rows_x), (3, rows_x), (4, 2), (4, 1)]
+    return pl.pallas_call(
+        split_kernel,
+        out_shape=[jax.ShapeDtypeStruct(shape + (LEVELS, WIDE), jnp.bfloat16) for shape in shapes],
+        in_specs=[smem, vmem],
+        out_specs=[vmem] * 5,
+        compiler_params=pltpu.CompilerParams(vmem_limit_bytes=16 * 1024 * 1024),
+        cost_estimate=pl.CostEstimate(flops=1_000_000, bytes_accessed=2_000_000, transcendentals=0),
+    )(flag, raw)
+
+
+def along_x_kernel(flags, face_x, own, xup, xdn, speeds_x, part):
     rows_x = own.shape[1]
     forward = flags[0] > 0
 
@@ -65,74 +105,84 @@
         lanes = pl.ds(pl.multiple_of(t * 128, 128), 128)
         nu_x = speeds_x[:, lanes]
         half_x = 0.5 * (1.0 - nu_x)
+        for q in range(4):
+            y = q // 2
+            far = xup[q, 0, :, lanes].astype(jnp.float32)
+            near = xup[q, 1, :, lanes].astype(jnp.float32)
+            now = own[q, pick(0), :, lanes].astype(jnp.float32)
+            diff = now - near
+            flux = face_x[0, y] * (nu_x * (near + half_x * minmod(near - far, diff)))
+            for step in range(rows_x):
+                if step + 1 < rows_x:
+                    nxt = own[q, pick(step + 1), :, lanes].astype(jnp.float32)
+                else:
+                    nxt = xdn[q, 0, :, lanes].astype(jnp.float32)
+                later = nxt - now
+                flux_out = face_x[step + 1, y] * (nu_x * (now + half_x * minmod(diff, later)))
+                part[q, pick(step), :, lanes] = now + (flux - flux_out)
+                now, diff, flux = nxt, later, flux_out
+        return carry
+
+    lax.fori_loop(0, WIDE // 128, tile, 0)
+
+
+def along_y_kernel(face_y, part, own, low, high_, speeds_y, out):
+    rows_x = own.shape[1]
+
+    def tile(t, carry):
+        lanes = pl.ds(pl.multiple_of(t * 128, 128), 128)
         for half in range(2):
             nu_y = speeds_y[half, :, lanes]
             half_y = 0.5 * (1.0 - nu_y)
-            first, second = (0, 1) if half == 1 else (1, 0)
-
-            def f32(ref, *at):
-                return ref[at[0], at[1], :, lanes].astype(jnp.float32)
-
-            prev = []
-            for y in range(2):
-                q = 2 * y + half
-                far = f32(xup, q, 0)
-                near = f32(xup, q, 1)
-                now = f32(own, q, pick(0))
-                slope = minmod(near - far, now - near)
-                flux = face_x[0, y] * (nu_x * (near + half_x * slope))
-                prev.append((now, now - near, flux))
-            for step in range(rows_x):
-                row = pick(step)
-                changed = []
-                values = []
-                for y in range(2):
-                    q = 2 * y + half
-                    now, diff, flux = prev[y]
-                    if step + 1 < rows_x:
-                        nxt = f32(own, q, pick(step + 1))
-                    else:
-                        nxt = f32(xdn, q, 0)
-                    later = nxt - now
-                    flux_out = face_x[step + 1, y] * (
-                        nu_x * (now + half_x * minmod(diff, later))
-                    )
-                    changed.append(now + (flux - flux_out))
-                    values.append(now)
-                    prev[y] = (nxt, later, flux_out)
+            first, second = (half, 2 + half) if half == 1 else (2 + half, half)
+            w0, w1, w2 = (0, 1, 2) if half == 1 else (2, 1, 0)
+            for row in range(rows_x):
+
+                def f32(ref, at):
+                    return ref[at, row, :, lanes].astype(jnp.float32)
+
                 if half == 1:
-                    up2, up1, down = f32(low, 0, row), f32(low, 1, row), f32(high_, 2, row)
+                    up2, up1, down = f32(low, 0), f32(low, 1), f32(high_, 2)
                 else:
-                    up2, up1, down = f32(high_, 1, row), f32(high_, 0, row), f32(low, 2, row)
-                a, b = values[first], values[second]
+                    up2, up1, down = f32(high_, 1), f32(high_, 0), f32(low, 2)
+                a, b = f32(own, first), f32(own, second)
                 d0, d1, d2, d3 = up1 - up2, a - up1, b - a, down - b
-                w0, w1, w2 = (0, 1, 2) if half == 1 else (2, 1, 0)
                 g0 = face_y[row, w0] * (nu_y * (up1 + half_y * minmod(d0, d1)))
                 g1 = face_y[row, w1] * (nu_y * (a + half_y * minmod(d1, d2)))
                 g2 = face_y[row, w2] * (nu_y * (b + half_y * minmod(d2, d3)))
-                out[row, 2 * first + half, :, lanes] = (changed[first] + (g0 - g1)).astype(
-                    jnp.bfloat16
-                )
-                out[row, 2 * second + half, :, lanes] = (changed[second] + (g1 - g2)).astype(
-                    jnp.bfloat16
-                )
+                for at, change in ((first, g0 - g1), (second, g1 - g2)):
+                    value = part[at, row, :, lanes] + change
+                    out[row, at, :, lanes] = value.astype(jnp.bfloat16)
         return carry
 
     lax.fori_loop(0, WIDE // 128, tile, 0)
 
 
-def transport(flag, face_x, face_y, own, xup, xdn, low, high_, speeds_x, speeds_y):
+def along_x(flag, face_x, own, xup, xdn, speeds_x):
+    smem = pl.BlockSpec(memory_space=pltpu.SMEM)
+    vmem = pl.BlockSpec(memory_space=pltpu.VMEM)
+    return pl.pallas_call(
+        along_x_kernel,
+        out_shape=jax.ShapeDtypeStruct(own.shape, jnp.float32),
+        in_specs=[smem] * 2 + [vmem] * 4,
+        out_specs=vmem,
+        compiler_params=pltpu.CompilerParams(vmem_limit_bytes=16 * 1024 * 1024),
+        cost_estimate=pl.CostEstimate(flops=5_000_000, bytes_accessed=1_500_000, transcendentals=0),
+    )(flag, face_x, own, xup, xdn, speeds_x)
+
+
+def along_y(face_y, part, own, low, high_, speeds_y):
     rows_x = own.shape[1]
     smem = pl.BlockSpec(memory_space=pltpu.SMEM)
     vmem = pl.BlockSpec(memory_space=pltpu.VMEM)
     return pl.pallas_call(
-        transport_kernel,
+        along_y_kernel,
         out_shape=jax.ShapeDtypeStruct((rows_x, 4, LEVELS, WIDE), jnp.bfloat16),
-        in_specs=[smem] * 3 + [vmem] * 7,
+        in_specs=[smem] + [vmem] * 5,
         out_specs=vmem,
         compiler_params=pltpu.CompilerParams(vmem_limit_bytes=16 * 1024 * 1024),
-        cost_estimate=pl.CostEstimate(flops=10_000_000, bytes_accessed=2_000_000, transcendentals=0),
-    )(flag, face_x, face_y, own, xup, xdn, low, high_, speeds_x, speeds_y)
+        cost_estimate=pl.CostEstimate(flops=5_000_000, bytes_accessed=2_500_000, transcendentals=0),
+    )(face_y, part, own, low, high_, speeds_y)
 
 
 def small(matrix, inputs):
@@ -308,17 +358,17 @@
         )
 
     for direction in range(2):
-        prepare_all(0, direction, spec)
-        prepare_all(1, 2 + direction, mixed)
+        prepare_all(2 * direction, direction, spec)
+        prepare_all(2 * direction + 1, 2 + direction, mixed)
         for start, width in chunks:
-            left[:, pl.ds(start, width)] = product(0, start, width)
+            left[:, pl.ds(start, width)] = product(2 * direction, start, width)
         for start, width in chunks:
             cols = pl.ds(start, width)
-            value = left[:, cols] * product(1, start, width)
+            value = left[:, cols] * product(2 * direction + 1, start, width)
             gain[:, cols] = value if direction == 0 else gain[:, cols] + value
-    prepare_all(0, 4, mixed)
+    prepare_all(4, 4, mixed)
     for start, width in chunks:
-        loss = product(0, start, width)
+        loss = product(4, start, width)
         for cell in range(cells):
             at_rows = pl.ds(cell * per_cell, per_cell)
             keep = min(width, PLANE - start)
@@ -343,7 +393,7 @@
             pltpu.VMEM((count, YZ), jnp.bfloat16),
             pltpu.VMEM((count, YZ), jnp.float32),
             pltpu.VMEM((count, YZ), jnp.float32),
-            pltpu.VMEM((2, count, DEPTH), jnp.bfloat16),
+            pltpu.VMEM((5, count, DEPTH), jnp.bfloat16),
             pltpu.VMEM((count, YZ), jnp.float32),
             pltpu.VMEM((count, YZ), jnp.float32),
         ],
@@ -366,12 +416,12 @@
     at_v = lax.axis_index("vert")
     forward = at_v >= count_v // 2
 
-    own = distribution.reshape(rows_x, 2, SUB, LEVELS, 2, HALF)
-    own = own.transpose(1, 4, 0, 3, 2, 5).reshape(4, rows_x, LEVELS, LANES)
-    own = jnp.pad(own, ((0, 0), (0, 0), (0, 0), (0, WIDE - LANES)))
-
-    low = lax.ppermute(jnp.stack([own[1], own[3], own[2]]), "gy", ring(count_y, 1))
-    high_ = lax.ppermute(jnp.stack([own[0], own[2], own[1]]), "gy", ring(count_y, -1))
+    flag = forward.astype(jnp.int32).reshape(1)
+    raw = distribution.transpose(0, 2, 1, 3).reshape(rows_x, SUB, 2, LEVELS, PLANE)
+    own, to_low, to_high, upstream, downstream = split(flag, raw)
+    low = lax.ppermute(to_high, "gy", ring(count_y, 1))
+    high_ = lax.ppermute(to_low, "gy", ring(count_y, -1))
+
     openness = open_share(wall_mask)
     wrapped = jnp.pad(openness, 1, mode="wrap")
     anchor_x = lax.axis_index("gx") * rows_x
@@ -382,9 +432,9 @@
     face_x = jnp.where(forward, face_x, face_x[::-1])
     open_y = window[1 : rows_x + 1]
     face_y = jnp.minimum(open_y[:, :-1], open_y[:, 1:])
-    own_x, face_x, face_y = lax.optimization_barrier((own, face_x, face_y))
-    upstream = jnp.where(forward, own_x[:, rows_x - 2 :], own_x[:, 1::-1])
-    downstream = jnp.where(forward, own_x[:, :1], own_x[:, rows_x - 1 :])
+    upstream, downstream, face_x, face_y = lax.optimization_barrier(
+        (upstream, downstream, face_x, face_y)
+    )
     send_up, send_down = [], []
     for i in range(count_x):
         for v in range(count_v):
@@ -400,8 +450,8 @@
     speeds_x = jnp.abs(speed(index_x.astype(jnp.float32)))
     speeds_x = jnp.broadcast_to(speeds_x[None], (LEVELS, WIDE))
     speeds_y = jnp.asarray(lane_speeds())
-    flag = forward.astype(jnp.int32).reshape(1)
-    transported = transport(flag, face_x, face_y, own, xup, xdn, low, high_, speeds_x, speeds_y)
+    part = along_x(flag, face_x, own, xup, xdn, speeds_x)
+    transported = along_y(face_y, part, own, low, high_, speeds_y)
 
     block = lax.all_to_all(transported, "vert", split_axis=0, concat_axis=0, tiled=True)
     entries = jnp.arange(trans_weight.shape[0], dtype=jnp.int32)

time: 83.3 us -> 83.5 us (level)
  waiting for transfers between devices: 15.5 us -> 16.5 us
    unnamed x19, local copies, waits for them, and re-layouts: 1.16 us -> 2.8 us
    reshape x3 -> x1, local copies, waits for them, and re-layouts: 2.82 us -> 1.48 us  [body(): distribution.transpose(0, 2, 1, 3).reshape(rows_x, SUB, 2, LEVELS, PLANE)]
    reshape x1, local copies, waits for them, and re-layouts: 1.13 us -> 0.11 us  [body(): bank = kernels.reshape(kernels.shape[0], VX, PLANE)[:, :VX // 2 + 1]]
    all_to_all x1, waiting for transfers between devices: 14.3 us -> 15.3 us  [body(): lax.all_to_all(transported, 'vert', split_axis=0, concat_axis=0, tiled=True)]
    pallas_call x1, Pallas kernels: 9.54 us -> 8.66 us  [collide(): pl.pallas_call(collide_kernel, out_shape=jax.ShapeDtypeStruct((count, PLA...]
    pallas_call x1 -> x3, Pallas kernels: 2.66 us -> 3.47 us  [the longest x1 2.07 us: along_y(): pl.pallas_call(along_y_kernel, out_shape=jax.ShapeDtypeStruct((rows_x, 4,...]
  transfers between devices with their start and end apart: 5 -> 5, of which waited for: 2 -> 2; matrix products, arithmetic and copies ran while one was open for 3% -> 3% of each run, Pallas kernels for 0% -> 1%
where the time goes in v2:
time: 83.5 us; the launch traced here: 82 us
  starting transfers between devices  27.8 us (33%)
  blocking collectives  18.6 us (22%)
  waiting for transfers between devices  16.5 us (20%)
  Pallas kernels  12.1 us (14%)
  local copies, waits for them, and re-layouts  5.41 us (6%)
  other arithmetic  1.35 us (2%)
    all_to_all x1, blocking collectives, body(): lax.all_to_all(updated, 'vert', split_axis=2, concat_axis=0, tiled=True)  18.6 us
    all_to_all x1, waiting for transfers between devices, body(): lax.all_to_all(transported, 'vert', split_axis=0, concat_axis=0, tiled=True)  15.3 us
    pallas_call x1, Pallas kernels, collide(): pl.pallas_call(collide_kernel, out_shape=jax.ShapeDtypeStruct((count, PLA...  8.66 us
    ppermute x1, starting transfers between devices, body(): high_ = lax.ppermute(to_low, 'gy', ring(count_y, -1))  8.59 us
    all_to_all x1, starting transfers between devices, body(): lax.all_to_all(transported, 'vert', split_axis=0, concat_axis=0, tiled=True)  8.46 us
    ppermute x1, starting transfers between devices, body(): low = lax.ppermute(to_high, 'gy', ring(count_y, 1))  4 us
    ppermute x1, starting transfers between devices, body(): xdn = lax.ppermute(downstream, ('gx', 'vert'), send_down)  3.91 us
    ppermute x1, starting transfers between devices, body(): xup = lax.ppermute(upstream, ('gx', 'vert'), send_up)  2.86 us
  transfers between devices with their start and end apart: 5, of which 2 were waited for; matrix products, arithmetic and copies ran while one was open for 3% of the time, Pallas kernels for 1%

profile of v2, /device:TPU:7, one launch (start us, length us, event | category | flops | bytes accessed | tf_op | source)
XLA Modules:
  0.0 82.0 jit_solution(9382114435882896502)
XLA Ops:
  0.0 0.0 copy-start
  0.0 1.5 %reshape.41.raw = bf16[8,3,2,8,576]{4,3,2,1,0:T(8,128)(2,1)S(1)} reshape(bf16[8,3,2,4608]{3,2,1,0:T(2,128)(2,1)} %bitcast.8) | data formatting | bytes 884736 | tf_op jit(solution)/shard_map/reshape | solution.py:420
  1.5 0.2 shard_map.91
  1.7 4.0 %collective-permute-start.2 = (bf16[3,8,8,896]{3,2,1,0:T(8,128)(2,1)S(1)}, bf16[3,8,8,896]{3,2,1,0:T(8,128)(2,1)S(1)}, u32[]{:S(2)}, u32[]{:S(2)}) collective-permute-start(bf16[3,8,8,896]{3,2,1,0:T(8,128)(2,1)S(1)} %get-tuple-element.21), channel_id=1, source_target_pairs={{0,8},{8,16},{16,24},{24,32},{32,40},{40,48},{48,56},{56,0},{1,9},... | collective-permute-start | bytes 1032200 | tf_op jit(solution)/shard_map/ppermute | solution.py:422
  5.7 8.6 %collective-permute-start.3 = (bf16[3,8,8,896]{3,2,1,0:T(8,128)(2,1)S(1)}, bf16[3,8,8,896]{3,2,1,0:T(8,128)(2,1)S(1)}, u32[]{:S(2)}, u32[]{:S(2)}) collective-permute-start(bf16[3,8,8,896]{3,2,1,0:T(8,128)(2,1)S(1)} %get-tuple-element.22), channel_id=1, source_target_pairs={{0,56},{8,0},{16,8},{24,16},{32,24},{40,32},{48,40},{56,48},{1,57}... | collective-permute-start | bytes 1032200 | tf_op jit(solution)/shard_map/ppermute | solution.py:423
  14.3 0.7 select_select_fusion
  15.0 0.1 fusion.17
  15.1 0.1 fusion.12
  15.2 0.1 fusion.18
  15.3 0.1 fusion.19
  15.3 0.1 copy.26
  15.4 0.1 copy.27
  15.6 0.1 copy.28
  15.6 0.1 copy.29
  15.7 2.9 %collective-permute-start = (bf16[4,2,8,896]{3,2,1,0:T(8,128)(2,1)S(1)}, bf16[4,2,8,896]{3,2,1,0:T(8,128)(2,1)S(1)}, u32[]{:S(2)}, u32[]{:S(2)}) collective-permute-start(bf16[4,2,8,896]{3,2,1,0:T(8,128)(2,1)S(1)} %get-tuple-element.19), channel_id=1, source_target_pairs={{0,448},{1,449},{2,450},{3,451},{4,68},{5,69},{6,70},{7,71},{64,0}... | collective-permute-start | bytes 344072 | tf_op jit(solution)/shard_map/ppermute | solution.py:444
  18.6 3.9 %collective-permute-start.1 = (bf16[4,1,8,896]{3,2,1,0:T(8,128)(2,1)S(1)}, bf16[4,1,8,896]{3,2,1,0:T(8,128)(2,1)S(1)}, u32[]{:S(2)}, u32[]{:S(2)}) collective-permute-start(bf16[4,1,8,896]{3,2,1,0:T(8,128)(2,1)S(1)} %get-tuple-element.20), channel_id=1, source_target_pairs={{0,64},{1,65},{2,66},{3,67},{4,452},{5,453},{6,454},{7,455},{64,12... | collective-permute-start | bytes 172040 | tf_op jit(solution)/shard_map/ppermute | solution.py:445
  22.5 1.2 %collective-permute-done.1.xdn = bf16[4,1,8,896]{3,2,1,0:T(8,128)(2,1)S(1)} collective-permute-done((bf16[4,1,8,896]{3,2,1,0:T(8,128)(2,1)S(1)}, bf16[4,1,8,896]{3,2,1,0:T(8,128)(2,1)S(1)}, u32[]{:S(2)}, u32[]{:S(2)}) %collective-permute-start.1) | collective-permute-done | bytes 57376 | tf_op jit(solution)/shard_map/ppermute | solution.py:445
  23.8 0.0 collective-permute-done.xup
  23.8 0.0 copy-start.2
  23.8 1.2 %shard_map.92.part = f32[4,8,8,896]{3,2,1,0:T(8,128)S(1)} custom-call(s32[1]{0:T(128)} %bitcast.flags, f32[9,2]{1,0:T(8,128)S(1)} %broadcast_select_fusion.face_x, bf16[4,8,8,896]{3,2,1,0:T(8,128)(2,1)S(1)} %get-tuple-element.18.own, bf16[4,2,8,896]{3,2,1,0:T(8,128)(2,1)S(1)} %collective-permute-done.xup, ...), custom_call_target="tpu_custom_call" | custom-call | flops 5000000 | bytes 1500000 | tf_op jit(solution)/shard_map/pallas_call | solution.py:164
  25.0 0.0 copy-start.5
  25.0 0.0 copy-start.4
  25.0 0.0 copy-start.6
  25.0 0.0 copy-start.3
  25.0 0.0 collective-permute-done.2.low
  25.0 0.0 collective-permute-done.3.high_
  25.0 0.0 copy-done
  25.0 2.1 %shard_map.93 = bf16[8,4,8,896]{3,2,1,0:T(8,128)(2,1)} custom-call(f32[8,3]{1,0:T(8,128)S(1)} %min.7.face_y, f32[4,8,8,896]{3,2,1,0:T(8,128)S(1)} %shard_map.92.part, bf16[4,8,8,896]{3,2,1,0:T(8,128)(2,1)S(1)} %get-tuple-element.18.own, bf16[3,8,8,896]{3,2,1,0:T(8,128)(2,1)S(1)} %collective-permute-done.2.low, ...), custom_call_target="tpu_custom_call" | custom-call | flops 5000000 | bytes 2500000 | tf_op jit(solution)/shard_map/pallas_call | solution.py:178
  27.1 8.5 %all-to-all-start = ((bf16[8,4,8,896]{3,2,1,0:T(8,128)(2,1)}), bf16[8,4,8,896]{3,2,1,0:T(8,128)(2,1)S(1)}, u32[]{:S(2)}, u32[]{:S(2)}) async-start(bf16[8,4,8,896]{3,2,1,0:T(8,128)(2,1)} %shard_map.93), calls=%async_computation | async-start | bytes 917504 | tf_op jit(solution)/shard_map/all_to_all | solution.py:456
  35.6 0.0 copy-done.2
  35.6 0.1 reshape.42
  35.7 0.0 copy-done.5
  35.7 0.1 slice_multiply_fusion
  35.8 0.2 multiply_reduce_fusion.weights
  36.0 0.0 copy-done.4
  36.0 0.0 copy-done.6
  36.0 0.2 select_reduce_fusion.1
  36.2 0.0 copy-done.3
  36.2 0.1 select_reduce_fusion
  36.3 15.3 %all-to-all-done.block = bf16[8,4,8,896]{3,2,1,0:T(8,128)(2,1)S(1)} async-done(((bf16[8,4,8,896]{3,2,1,0:T(8,128)(2,1)}), bf16[8,4,8,896]{3,2,1,0:T(8,128)(2,1)S(1)}, u32[]{:S(2)}, u32[]{:S(2)}) %all-to-all-start) | async-done | bytes 458784 | tf_op jit(solution)/shard_map/all_to_all | solution.py:456
  51.6 0.1 broadcast_in_dim.57.coefs
  51.7 0.0 copy-start.1
  51.7 1.6 %copy-done.1 = bf16[1792,640]{1,0:T(8,128)(2,1)S(1)} copy-done((bf16[1792,640]{1,0:T(8,128)(2,1)S(1)}, bf16[1792,640]{1,0:T(8,128)(2,1)}, u32[]{:S(2)}) %copy-start.1) | copy-done | bytes 2293784
  53.3 8.7 %shard_map.94 = bf16[384,576]{1,0:T(8,128)(2,1)S(1)} custom-call(f32[2]{0:T(128)S(1)} %multiply_reduce_fusion.weights, bf16[8,4,8,896]{3,2,1,0:T(8,128)(2,1)S(1)} %all-to-all-done.block, f32[5,13,640]{2,1,0:T(8,128)S(1)} %pad.4.bank, f32[8,8,128]{2,1,0:T(8,128)S(1)} %broadcast_in_dim.57.coefs, bf16[1792,640]{1,0:T(8,128)(2,1)S(1)} %copy-done.1), custom_call_target="tpu_custom_call" | custom-call | flops 8000000000 | bytes 8000000 | tf_op jit(solution)/shard_map/pallas_call | solution.py:387
  62.0 0.3 reshape.43
  62.3 0.3 copy.24
  62.7 18.6 %all_to_all.23 = bf16[1,2,24,4608]{3,1,0,2:T(2,128)(2,1)S(1)} all-to-all(bf16[1,2,24,4608]{3,1,0,2:T(2,128)(2,1)S(1)} %copy.24), channel_id=1, replica_groups=mesh['gx'=8,'gy'=8,'vert'=8] {'vert'}, dimensions={2} | all-to-all | bytes 884736 | tf_op jit(solution)/shard_map/all_to_all | solution.py:477
  81.3 0.8 copy.31
  (7 shorter events, 0.1 us)
Async XLA Ops:
  0.0 25.0 %copy-start = (f32[2,8,896]{2,1,0:T(8,128)S(1)}, f32[2,8,896]{2,1,0:T(8,128)}, u32[]{:S(2)}) copy-start(f32[2,8,896]{2,1,0:T(8,128)} %constant.67.clone.speeds_y) | copy-start | bytes 172036
  1.7 23.3 %collective-permute-start.2 = (bf16[3,8,8,896]{3,2,1,0:T(8,128)(2,1)S(1)}, bf16[3,8,8,896]{3,2,1,0:T(8,128)(2,1)S(1)}, u32[]{:S(2)}, u32[]{:S(2)}) collective-permute-start(bf16[3,8,8,896]{3,2,1,0:T(8,128)(2,1)S(1)} %get-tuple-element.21), channel_id=1, source_target_pairs={{0,8},{8,16},{16,24},{24,32},{32,40},{40,48},{48,56},{56,0},{1,9},... | collective-permute-start | bytes 1032200 | tf_op jit(solution)/shard_map/ppermute | solution.py:422
  5.7 19.3 %collective-permute-start.3 = (bf16[3,8,8,896]{3,2,1,0:T(8,128)(2,1)S(1)}, bf16[3,8,8,896]{3,2,1,0:T(8,128)(2,1)S(1)}, u32[]{:S(2)}, u32[]{:S(2)}) collective-permute-start(bf16[3,8,8,896]{3,2,1,0:T(8,128)(2,1)S(1)} %get-tuple-element.22), channel_id=1, source_target_pairs={{0,56},{8,0},{16,8},{24,16},{32,24},{40,32},{48,40},{56,48},{1,57}... | collective-permute-start | bytes 1032200 | tf_op jit(solution)/shard_map/ppermute | solution.py:423
  15.7 8.0 %collective-permute-start = (bf16[4,2,8,896]{3,2,1,0:T(8,128)(2,1)S(1)}, bf16[4,2,8,896]{3,2,1,0:T(8,128)(2,1)S(1)}, u32[]{:S(2)}, u32[]{:S(2)}) collective-permute-start(bf16[4,2,8,896]{3,2,1,0:T(8,128)(2,1)S(1)} %get-tuple-element.19), channel_id=1, source_target_pairs={{0,448},{1,449},{2,450},{3,451},{4,68},{5,69},{6,70},{7,71},{64,0}... | collective-permute-start | bytes 344072 | tf_op jit(solution)/shard_map/ppermute | solution.py:444
  18.6 5.2 %collective-permute-start.1 = (bf16[4,1,8,896]{3,2,1,0:T(8,128)(2,1)S(1)}, bf16[4,1,8,896]{3,2,1,0:T(8,128)(2,1)S(1)}, u32[]{:S(2)}, u32[]{:S(2)}) collective-permute-start(bf16[4,1,8,896]{3,2,1,0:T(8,128)(2,1)S(1)} %get-tuple-element.20), channel_id=1, source_target_pairs={{0,64},{1,65},{2,66},{3,67},{4,452},{5,453},{6,454},{7,455},{64,12... | collective-permute-start | bytes 172040 | tf_op jit(solution)/shard_map/ppermute | solution.py:445
  23.8 11.8 %copy-start.2 = (f32[5,13824]{1,0:T(8,128)S(1)}, f32[5,13824]{1,0:T(8,128)}, u32[]{:S(2)}) copy-start(f32[5,13824]{1,0:T(8,128)} %param.13) | copy-start | bytes 829444
  25.0 10.7 %copy-start.5 = (f32[13]{0:T(128)S(1)}, f32[13]{0:T(128)}, u32[]{:S(2)}) copy-start(f32[13]{0:T(128)} %constant.74) | copy-start | bytes 160
  25.0 11.1 %copy-start.4 = (s32[8,8]{1,0:T(8,128)S(1)}, s32[8,8]{1,0:T(8,128)}, u32[]{:S(2)}) copy-start(s32[8,8]{1,0:T(8,128)} %param.11) | copy-start | bytes 772
  25.0 11.0 %copy-start.6 = (f32[8]{0:T(128)S(1)}, f32[8]{0:T(128)}, u32[]{:S(2)}) copy-start(f32[8]{0:T(128)} %param.12) | copy-start | bytes 100
  25.0 11.2 %copy-start.3 = (pred[8,8,8]{2,1,0:T(8,128)(4,1)S(1)}, pred[8,8,8]{2,1,0:T(8,128)(4,1)}, u32[]{:S(2)}) copy-start(pred[8,8,8]{2,1,0:T(8,128)(4,1)} %constant.68.clone) | copy-start | bytes 1540
  27.1 24.5 %all-to-all-start = ((bf16[8,4,8,896]{3,2,1,0:T(8,128)(2,1)}), bf16[8,4,8,896]{3,2,1,0:T(8,128)(2,1)S(1)}, u32[]{:S(2)}, u32[]{:S(2)}) async-start(bf16[8,4,8,896]{3,2,1,0:T(8,128)(2,1)} %shard_map.93), calls=%async_computation | async-start | bytes 917504 | tf_op jit(solution)/shard_map/all_to_all | solution.py:456
  51.7 1.7 %copy-start.1 = (bf16[1792,640]{1,0:T(8,128)(2,1)S(1)}, bf16[1792,640]{1,0:T(8,128)(2,1)}, u32[]{:S(2)}) copy-start(bf16[1792,640]{1,0:T(8,128)(2,1)} %constant.70.clone.back) | copy-start | bytes 6881284

commit v3 on v2

--- a/solution.py
+++ b/solution.py
@@ -9,6 +9,8 @@
 from jax.experimental.pallas import tpu as pltpu
 from jax.sharding import PartitionSpec as P
 
+NX = 64
+NY = 16
 VX = 24
 VY = 24
 VZ = 24
@@ -20,7 +22,7 @@
 WIDE = 896
 YZ = 640
 MAIN = 512
-DEPTH = 3 * MAIN + 256
+DEPTH = 2 * MAIN + 256
 HIGH_ORDER = (1, 3, 2)
 LOW_ORDER = (0, 2, 1)
 
@@ -56,7 +58,7 @@
     return jnp.maximum(jnp.minimum(a, b), jnp.minimum(jnp.maximum(a, b), 0.0))
 
 
-def split_kernel(flags, raw, own, to_low, to_high, to_down, to_up):
+def split_kernel(raw, own, to_low, to_high):
     rows_x = raw.shape[0]
     blank = jnp.zeros((LEVELS, WIDE - LANES), jnp.float32)
     for x in range(rows_x):
@@ -71,6 +73,10 @@
                     to_high[HIGH_ORDER.index(q), x] = value
                 if q in LOW_ORDER:
                     to_low[LOW_ORDER.index(q), x] = value
+
+
+def edges_kernel(flags, own, to_down, to_up):
+    rows_x = own.shape[1]
     forward = flags[0] > 0
     for q in range(4):
         for step in range(2):
@@ -79,27 +85,51 @@
         to_up[q, 0] = own[q, jnp.where(forward, 0, rows_x - 1)]
 
 
-def split(flag, raw):
-    rows_x = raw.shape[0]
+def edges(flag, own):
     smem = pl.BlockSpec(memory_space=pltpu.SMEM)
     vmem = pl.BlockSpec(memory_space=pltpu.VMEM)
-    shapes = [(4, rows_x), (3, rows_x), (3, rows_x), (4, 2), (4, 1)]
+    return pl.pallas_call(
+        edges_kernel,
+        out_shape=[
+            jax.ShapeDtypeStruct((4, count, LEVELS, WIDE), jnp.bfloat16) for count in (2, 1)
+        ],
+        in_specs=[smem, vmem],
+        out_specs=[vmem] * 2,
+        compiler_params=pltpu.CompilerParams(vmem_limit_bytes=8 * 1024 * 1024),
+        cost_estimate=pl.CostEstimate(flops=100_000, bytes_accessed=400_000, transcendentals=0),
+    )(flag, own)
+
+
+def split(raw):
+    rows_x = raw.shape[0]
+    vmem = pl.BlockSpec(memory_space=pltpu.VMEM)
+    shapes = [(4, rows_x), (3, rows_x), (3, rows_x)]
     return pl.pallas_call(
         split_kernel,
         out_shape=[jax.ShapeDtypeStruct(shape + (LEVELS, WIDE), jnp.bfloat16) for shape in shapes],
-        in_specs=[smem, vmem],
-        out_specs=[vmem] * 5,
-        compiler_params=pltpu.CompilerParams(vmem_limit_bytes=16 * 1024 * 1024),
+        in_specs=[vmem],
+        out_specs=[vmem] * 3,
+        compiler_params=pltpu.CompilerParams(vmem_limit_bytes=8 * 1024 * 1024),
         cost_estimate=pl.CostEstimate(flops=1_000_000, bytes_accessed=2_000_000, transcendentals=0),
-    )(flag, raw)
-
-
-def along_x_kernel(flags, face_x, own, xup, xdn, speeds_x, part):
+    )(raw)
+
+
+def open_at(mask, row, column):
+    flag = mask[lax.rem(row + NX, NX), lax.rem(column + NY, NY)]
+    return jnp.where(flag == 1, 0.0, jnp.where(flag == 2, 0.5, 1.0)).astype(jnp.float32)
+
+
+def along_x_kernel(flags, mask, own, xup, xdn, speeds_x, part, face_x):
     rows_x = own.shape[1]
     forward = flags[0] > 0
 
     def pick(step):
         return jnp.where(forward, step, rows_x - 1 - step)
+
+    for y in range(2):
+        cells = [open_at(mask, flags[1] + pick(step), flags[2] + y) for step in range(-1, rows_x + 1)]
+        for step in range(rows_x + 1):
+            face_x[step, y] = jnp.minimum(cells[step], cells[step + 1])
 
     def tile(t, carry):
         lanes = pl.ds(pl.multiple_of(t * 128, 128), 128)
@@ -126,8 +156,12 @@
     lax.fori_loop(0, WIDE // 128, tile, 0)
 
 
-def along_y_kernel(face_y, part, own, low, high_, speeds_y, out):
+def along_y_kernel(flags, mask, part, own, low, high_, speeds_y, out, face_y):
     rows_x = own.shape[1]
+    for row in range(rows_x):
+        cells = [open_at(mask, flags[1] + row, flags[2] + y) for y in range(-1, 3)]
+        for face in range(3):
+            face_y[row, face] = jnp.minimum(cells[face], cells[face + 1])
 
     def tile(t, carry):
         lanes = pl.ds(pl.multiple_of(t * 128, 128), 128)
@@ -158,7 +192,7 @@
     lax.fori_loop(0, WIDE // 128, tile, 0)
 
 
-def along_x(flag, face_x, own, xup, xdn, speeds_x):
+def along_x(flag, mask, own, xup, xdn, speeds_x):
     smem = pl.BlockSpec(memory_space=pltpu.SMEM)
     vmem = pl.BlockSpec(memory_space=pltpu.VMEM)
     return pl.pallas_call(
@@ -166,23 +200,25 @@
         out_shape=jax.ShapeDtypeStruct(own.shape, jnp.float32),
         in_specs=[smem] * 2 + [vmem] * 4,
         out_specs=vmem,
-        compiler_params=pltpu.CompilerParams(vmem_limit_bytes=16 * 1024 * 1024),
+        scratch_shapes=[pltpu.SMEM((own.shape[1] + 1, 2), jnp.float32)],
+        compiler_params=pltpu.CompilerParams(vmem_limit_bytes=8 * 1024 * 1024),
         cost_estimate=pl.CostEstimate(flops=5_000_000, bytes_accessed=1_500_000, transcendentals=0),
-    )(flag, face_x, own, xup, xdn, speeds_x)
-
-
-def along_y(face_y, part, own, low, high_, speeds_y):
+    )(flag, mask, own, xup, xdn, speeds_x)
+
+
+def along_y(flag, mask, part, own, low, high_, speeds_y):
     rows_x = own.shape[1]
     smem = pl.BlockSpec(memory_space=pltpu.SMEM)
     vmem = pl.BlockSpec(memory_space=pltpu.VMEM)
     return pl.pallas_call(
         along_y_kernel,
         out_shape=jax.ShapeDtypeStruct((rows_x, 4, LEVELS, WIDE), jnp.bfloat16),
-        in_specs=[smem] + [vmem] * 5,
+        in_specs=[smem] * 2 + [vmem] * 5,
         out_specs=vmem,
-        compiler_params=pltpu.CompilerParams(vmem_limit_bytes=16 * 1024 * 1024),
+        scratch_shapes=[pltpu.SMEM((rows_x, 3), jnp.float32)],
+        compiler_params=pltpu.CompilerParams(vmem_limit_bytes=8 * 1024 * 1024),
         cost_estimate=pl.CostEstimate(flops=5_000_000, bytes_accessed=2_500_000, transcendentals=0),
-    )(face_y, part, own, low, high_, speeds_y)
+    )(flag, mask, part, own, low, high_, speeds_y)
 
 
 def small(matrix, inputs):
@@ -265,11 +301,10 @@
     rest = PLANE - MAIN
     back = np.zeros((DEPTH, YZ), ml_dtypes.bfloat16)
     back[0:MAIN] = top[:MAIN]
-    back[MAIN : 2 * MAIN] = top[:MAIN]
-    back[2 * MAIN : 3 * MAIN] = low[:MAIN]
-    back[3 * MAIN : 3 * MAIN + rest] = top[MAIN:PLANE]
-    back[3 * MAIN + rest : 3 * MAIN + 2 * rest] = top[MAIN:PLANE]
-    back[3 * MAIN + 128 : 3 * MAIN + 128 + rest] = low[MAIN:PLANE]
+    back[MAIN : 2 * MAIN] = low[:MAIN]
+    back[2 * MAIN : 2 * MAIN + rest] = top[MAIN:PLANE]
+    back[2 * MAIN + rest : 2 * MAIN + 2 * rest] = top[MAIN:PLANE]
+    back[2 * MAIN + 128 : 2 * MAIN + 128 + rest] = low[MAIN:PLANE]
     return back
 
 
@@ -298,8 +333,8 @@
     edge = jnp.concatenate([g[:, MAIN:], g[:, MAIN:]], axis=1)
     for start, width in chunks:
         cols = pl.ds(start, width)
-        total = jnp.dot(edge, back[3 * MAIN :, cols], preferred_element_type=jnp.float32)
-        for first in (0, 2 * MAIN):
+        total = jnp.dot(edge, back[2 * MAIN :, cols], preferred_element_type=jnp.float32)
+        for first in (0, MAIN):
             total = total + jnp.dot(
                 g[:, :MAIN], back[pl.ds(first, MAIN), cols], preferred_element_type=jnp.float32
             )
@@ -308,13 +343,17 @@
     def rows(base, a, count=LEVELS):
         return pl.ds(base + a * LEVELS, count)
 
+    factor = [
+        jnp.broadcast_to(coefs[:, shift : shift + 1], (LEVELS, 128)) for shift in range(LEVELS)
+    ]
+
     def ahead(index):
         base, lanes = index // tiles * per_cell, pl.ds(index % tiles * 128, 128)
         modes = modes_of([spec[rows(base, a), lanes] for a in range(VX)])
         for a in range(VX):
-            total = coefs[0] * modes[a]
+            total = factor[0] * modes[a]
             for shift in range(1, LEVELS):
-                total = total + coefs[shift] * pltpu.roll(modes[a], shift, 0)
+                total = total + factor[shift] * pltpu.roll(modes[a], shift, 0)
             spec[rows(base, a), lanes] = modes[a]
             mixed[rows(base, a), lanes] = total
 
@@ -339,12 +378,11 @@
 
             if last:
                 both = jnp.where(lane < PLANE - MAIN, pair, pltpu.roll(rest, 64, 1))
-                put(3 * MAIN, both.astype(jnp.bfloat16))
-                put(3 * MAIN + 128, top)
+                put(2 * MAIN, both.astype(jnp.bfloat16))
+                put(2 * MAIN + 128, top)
             else:
-                put(t * 128, top)
-                put(MAIN + t * 128, rest.astype(jnp.bfloat16))
-                put(2 * MAIN + t * 128, top)
+                put(t * 128, rest.astype(jnp.bfloat16))
+                put(MAIN + t * 128, top)
 
     def prepare_all(slot, which, source):
         for cell in range(cells):
@@ -353,9 +391,17 @@
                 prepare(slot, which, source, base, pl.ds(t * 128, 128), t, t == tiles - 1)
 
     def product(slot, start, width):
-        return jnp.dot(
-            lhs[slot], back[:, pl.ds(start, width)], preferred_element_type=jnp.float32
+        cols = pl.ds(start, width)
+        total = jnp.dot(
+            lhs[slot, :, MAIN:], back[MAIN:, cols], preferred_element_type=jnp.float32
         )
+        for first in (0, MAIN):
+            total = total + jnp.dot(
+                lhs[slot, :, pl.ds(first, MAIN)],
+                back[:MAIN, cols],
+                preferred_element_type=jnp.float32,
+            )
+        return total
 
     for direction in range(2):
         prepare_all(2 * direction, direction, spec)
@@ -378,6 +424,24 @@
                 gain[at_rows, pl.ds(start, width)] - fields * part
             )
             out[at_rows, pl.ds(start, keep)] = value[:, :keep].astype(jnp.bfloat16)
+
+
+def resident_kernel(source, out, sem):
+    copy = pltpu.make_async_copy(source, out, sem)
+    copy.start()
+    copy.wait()
+
+
+def resident(table):
+    return pl.pallas_call(
+        resident_kernel,
+        out_shape=jax.ShapeDtypeStruct(table.shape, table.dtype),
+        in_specs=[pl.BlockSpec(memory_space=pl.ANY)],
+        out_specs=pl.BlockSpec(memory_space=pltpu.VMEM),
+        scratch_shapes=[pltpu.SemaphoreType.DMA],
+        compiler_params=pltpu.CompilerParams(vmem_limit_bytes=8 * 1024 * 1024),
+        cost_estimate=pl.CostEstimate(flops=0, bytes_accessed=4_600_000, transcendentals=0),
+    )(table)
 
 
 def collide(weights, block, bank, coefs, back):
@@ -416,25 +480,17 @@
     at_v = lax.axis_index("vert")
     forward = at_v >= count_v // 2
 
-    flag = forward.astype(jnp.int32).reshape(1)
+    anchor_x = lax.axis_index("gx") * rows_x
+    anchor_y = lax.axis_index("gy") * rows_y
+    flag = jnp.stack([forward.astype(jnp.int32), anchor_x, anchor_y])
     raw = distribution.transpose(0, 2, 1, 3).reshape(rows_x, SUB, 2, LEVELS, PLANE)
-    own, to_low, to_high, upstream, downstream = split(flag, raw)
+    own, to_low, to_high = split(raw)
     low = lax.ppermute(to_high, "gy", ring(count_y, 1))
     high_ = lax.ppermute(to_low, "gy", ring(count_y, -1))
 
-    openness = open_share(wall_mask)
-    wrapped = jnp.pad(openness, 1, mode="wrap")
-    anchor_x = lax.axis_index("gx") * rows_x
-    anchor_y = lax.axis_index("gy") * rows_y
-    window = lax.dynamic_slice(wrapped, (anchor_x, anchor_y), (rows_x + 2, rows_y + 2))
-    open_x = window[:, 1 : rows_y + 1]
-    face_x = jnp.minimum(open_x[:-1], open_x[1:])
-    face_x = jnp.where(forward, face_x, face_x[::-1])
-    open_y = window[1 : rows_x + 1]
-    face_y = jnp.minimum(open_y[:, :-1], open_y[:, 1:])
-    upstream, downstream, face_x, face_y = lax.optimization_barrier(
-        (upstream, downstream, face_x, face_y)
-    )
+    index_x = at_v * local_vx + jnp.arange(WIDE, dtype=jnp.int32) // HALF
+    speeds_x = jnp.abs(speed(index_x.astype(jnp.float32)))
+    upstream, downstream = edges(flag, own)
     send_up, send_down = [], []
     for i in range(count_x):
         for v in range(count_v):
@@ -444,15 +500,15 @@
     xup = lax.ppermute(upstream, ("gx", "vert"), send_up)
     xdn = lax.ppermute(downstream, ("gx", "vert"), send_down)
 
+    openness = open_share(wall_mask)
     own_open = lax.dynamic_slice(openness, (anchor_x + at_v, anchor_y), (1, rows_y))[0]
 
-    index_x = at_v * local_vx + jnp.arange(WIDE, dtype=jnp.int32) // HALF
-    speeds_x = jnp.abs(speed(index_x.astype(jnp.float32)))
     speeds_x = jnp.broadcast_to(speeds_x[None], (LEVELS, WIDE))
     speeds_y = jnp.asarray(lane_speeds())
-    part = along_x(flag, face_x, own, xup, xdn, speeds_x)
-    transported = along_y(face_y, part, own, low, high_, speeds_y)
-
+    part = along_x(flag, wall_mask, own, xup, xdn, speeds_x)
+    transported = along_y(flag, wall_mask, part, own, low, high_, speeds_y)
+
+    back = jnp.asarray(split_table())
     block = lax.all_to_all(transported, "vert", split_axis=0, concat_axis=0, tiled=True)
     entries = jnp.arange(trans_weight.shape[0], dtype=jnp.int32)
     mixing = jnp.sum(
@@ -462,16 +518,15 @@
         axis=-1,
     )
     level = np.arange(LEVELS)
-    chosen = (level[None, :, None] - level[:, None, None]) % LEVELS == level[None, None, :]
-    coefs = jnp.sum(jnp.where(chosen, mixing[None], 0.0), axis=-1)
-    coefs = jnp.broadcast_to(coefs[:, :, None], (LEVELS, LEVELS, 128))
+    chosen = (level[:, None, None] - level[None, :, None]) % LEVELS == level[None, None, :]
+    coefs = jnp.sum(jnp.where(chosen, mixing[:, None, :], 0.0), axis=-1)
     bank = kernels.reshape(kernels.shape[0], VX, PLANE)[:, : VX // 2 + 1]
     twice = np.full((VX // 2 + 1,), 2.0, np.float32)
     twice[0] = twice[VX // 2] = 1.0
     bank = bank * (twice / float(VX * PLANE)).reshape(1, -1, 1)
     bank = jnp.pad(bank, ((0, 0), (0, 0), (0, YZ - PLANE)))
     updated = collide(
-        collide_step * own_open, block, bank, coefs, jnp.asarray(split_table())
+        collide_step * own_open, block, bank, coefs, back
     )
     updated = updated.reshape(1, 2, VX, row_width)
     return lax.all_to_all(updated, "vert", split_axis=2, concat_axis=0, tiled=True)

time: 83.5 us -> 82.3 us (0.986)
  local copies, waits for them, and re-layouts: 5.41 us -> 3.18 us
  Pallas kernels: 12.1 us -> 13.8 us
    unnamed x19 -> x18, local copies, waits for them, and re-layouts: 2.8 us -> 0.88 us
  transfers between devices with their start and end apart: 5 -> 5, of which waited for: 2 -> 2; matrix products, arithmetic and copies ran while one was open for 3% -> 1% of each run, Pallas kernels for 1% -> 3%
where the time goes in v3:
time: 82.3 us; the launch traced here: 80.8 us
  starting transfers between devices  28 us (34%)
  blocking collectives  18.6 us (23%)
  waiting for transfers between devices  16.4 us (20%)
  Pallas kernels  13.8 us (17%)
  local copies, waits for them, and re-layouts  3.18 us (4%)
    all_to_all x1, blocking collectives, body(): lax.all_to_all(updated, 'vert', split_axis=2, concat_axis=0, tiled=True)  18.6 us
    all_to_all x1, waiting for transfers between devices, body(): lax.all_to_all(transported, 'vert', split_axis=0, concat_axis=0, tiled=True)  15.3 us
    pallas_call x1, Pallas kernels, collide(): pl.pallas_call(collide_kernel, out_shape=jax.ShapeDtypeStruct((count, PLA...  8.71 us
    all_to_all x1, starting transfers between devices, body(): lax.all_to_all(transported, 'vert', split_axis=0, concat_axis=0, tiled=True)  8.61 us
    ppermute x1, starting transfers between devices, body(): high_ = lax.ppermute(to_low, 'gy', ring(count_y, -1))  8.59 us
    ppermute x1, starting transfers between devices, body(): low = lax.ppermute(to_high, 'gy', ring(count_y, 1))  4 us
    ppermute x1, starting transfers between devices, body(): xdn = lax.ppermute(downstream, ('gx', 'vert'), send_down)  3.91 us
    ppermute x1, starting transfers between devices, body(): xup = lax.ppermute(upstream, ('gx', 'vert'), send_up)  2.86 us
  transfers between devices with their start and end apart: 5, of which 2 were waited for; matrix products, arithmetic and copies ran while one was open for 1% of the time, Pallas kernels for 3%

profile of v3, /device:TPU:7, one launch (start us, length us, event | category | flops | bytes accessed | tf_op | source)
XLA Modules:
  0.0 80.8 jit_solution(3057970935797845827)
XLA Ops:
  0.0 0.0 copy-start.3
  0.0 0.0 copy-start
  0.0 1.5 %reshape.33.raw = bf16[8,3,2,8,576]{4,3,2,1,0:T(8,128)(2,1)S(1)} reshape(bf16[8,3,2,4608]{3,2,1,0:T(2,128)(2,1)} %bitcast.10) | data formatting | bytes 884736 | tf_op jit(solution)/shard_map/reshape | solution.py:486
  1.5 0.2 shard_map.91
  1.7 4.0 %collective-permute-start.2 = (bf16[3,8,8,896]{3,2,1,0:T(8,128)(2,1)S(1)}, bf16[3,8,8,896]{3,2,1,0:T(8,128)(2,1)S(1)}, u32[]{:S(2)}, u32[]{:S(2)}) collective-permute-start(bf16[3,8,8,896]{3,2,1,0:T(8,128)(2,1)S(1)} %get-tuple-element.13), channel_id=1, source_target_pairs={{0,8},{8,16},{16,24},{24,32},{32,40},{40,48},{48,56},{56,0},{1,9},... | collective-permute-start | bytes 1032200 | tf_op jit(solution)/shard_map/ppermute | solution.py:488
  5.7 8.6 %collective-permute-start.3 = (bf16[3,8,8,896]{3,2,1,0:T(8,128)(2,1)S(1)}, bf16[3,8,8,896]{3,2,1,0:T(8,128)(2,1)S(1)}, u32[]{:S(2)}, u32[]{:S(2)}) collective-permute-start(bf16[3,8,8,896]{3,2,1,0:T(8,128)(2,1)S(1)} %get-tuple-element.14), channel_id=1, source_target_pairs={{0,56},{8,0},{16,8},{24,16},{32,24},{40,32},{48,40},{56,48},{1,57}... | collective-permute-start | bytes 1032200 | tf_op jit(solution)/shard_map/ppermute | solution.py:489
  14.3 0.1 pad_add_fusion.flags
  14.4 0.6 shard_map.92
  14.9 2.9 %collective-permute-start = (bf16[4,2,8,896]{3,2,1,0:T(8,128)(2,1)S(1)}, bf16[4,2,8,896]{3,2,1,0:T(8,128)(2,1)S(1)}, u32[]{:S(2)}, u32[]{:S(2)}) collective-permute-start(bf16[4,2,8,896]{3,2,1,0:T(8,128)(2,1)S(1)} %get-tuple-element.11), channel_id=1, source_target_pairs={{0,448},{1,449},{2,450},{3,451},{4,68},{5,69},{6,70},{7,71},{64,0}... | collective-permute-start | bytes 344072 | tf_op jit(solution)/shard_map/ppermute | solution.py:500
  17.8 3.9 %collective-permute-start.1 = (bf16[4,1,8,896]{3,2,1,0:T(8,128)(2,1)S(1)}, bf16[4,1,8,896]{3,2,1,0:T(8,128)(2,1)S(1)}, u32[]{:S(2)}, u32[]{:S(2)}) collective-permute-start(bf16[4,1,8,896]{3,2,1,0:T(8,128)(2,1)S(1)} %get-tuple-element.12), channel_id=1, source_target_pairs={{0,64},{1,65},{2,66},{3,67},{4,452},{5,453},{6,454},{7,455},{64,12... | collective-permute-start | bytes 172040 | tf_op jit(solution)/shard_map/ppermute | solution.py:501
  21.7 0.0 copy-done.3
  21.7 0.1 copy.23.mask
  21.8 1.1 %collective-permute-done.1.xdn = bf16[4,1,8,896]{3,2,1,0:T(8,128)(2,1)S(1)} collective-permute-done((bf16[4,1,8,896]{3,2,1,0:T(8,128)(2,1)S(1)}, bf16[4,1,8,896]{3,2,1,0:T(8,128)(2,1)S(1)}, u32[]{:S(2)}, u32[]{:S(2)}) %collective-permute-start.1) | collective-permute-done | bytes 57376 | tf_op jit(solution)/shard_map/ppermute | solution.py:501
  23.0 0.0 collective-permute-done.xup
  23.0 1.7 %shard_map.93.part = f32[4,8,8,896]{3,2,1,0:T(8,128)S(1)} custom-call(s32[3]{0:T(128)S(1)} %pad_add_fusion.flags, s32[64,16]{1,0:T(8,128)S(1)} %copy.23.mask, bf16[4,8,8,896]{3,2,1,0:T(8,128)(2,1)S(1)} %get-tuple-element.10.own, bf16[4,2,8,896]{3,2,1,0:T(8,128)(2,1)S(1)} %collective-permute-done.xup, bf16[4,1,8,896]{3,2,1,0:T(8,128)(2,1)S(1)} %collective-permute-done.1.xdn, ...), custom_call_target="tpu_custom_call" | custom-call | flops 5000000 | bytes 1500000 | tf_op jit(solution)/shard_map/pallas_call | solution.py:198
  24.7 0.0 copy-start.2
  24.7 0.0 copy-start.6
  24.7 0.0 collective-permute-done.2.low
  24.7 0.0 collective-permute-done.3.high_
  24.7 0.0 copy-done
  24.7 2.7 %shard_map.94 = bf16[8,4,8,896]{3,2,1,0:T(8,128)(2,1)} custom-call(s32[3]{0:T(128)S(1)} %pad_add_fusion.flags, s32[64,16]{1,0:T(8,128)S(1)} %copy.23.mask, f32[4,8,8,896]{3,2,1,0:T(8,128)S(1)} %shard_map.93.part, bf16[4,8,8,896]{3,2,1,0:T(8,128)(2,1)S(1)} %get-tuple-element.10.own, bf16[3,8,8,896]{3,2,1,0:T(8,128)(2,1)S(1)} %collective-permute-done.2.low, ...), custom_call_target="tpu_custom_call" | custom-call | flops 5000000 | bytes 2500000 | tf_op jit(solution)/shard_map/pallas_call | solution.py:213
  27.4 0.0 copy-start.5
  27.4 0.0 copy-start.7
  27.4 0.0 copy-start.4
  27.4 0.0 copy-start.1
  27.4 8.6 %all-to-all-start = ((bf16[8,4,8,896]{3,2,1,0:T(8,128)(2,1)}), bf16[8,4,8,896]{3,2,1,0:T(8,128)(2,1)S(1)}, u32[]{:S(2)}, u32[]{:S(2)}) async-start(bf16[8,4,8,896]{3,2,1,0:T(8,128)(2,1)} %shard_map.94), calls=%async_computation | async-start | bytes 917504 | tf_op jit(solution)/shard_map/all_to_all | solution.py:512
  36.0 0.0 copy-done.2
  36.0 0.1 reshape.34
  36.1 0.0 copy-done.6
  36.2 0.1 slice_multiply_fusion
  36.3 0.2 fusion.10.weights
  36.5 0.0 copy-done.5
  36.5 0.0 copy-done.7
  36.5 0.2 select_reduce_fusion.1
  36.6 0.0 copy-done.4
  36.6 0.1 select_reduce_fusion.coefs
  36.7 15.3 %all-to-all-done.block = bf16[8,4,8,896]{3,2,1,0:T(8,128)(2,1)S(1)} async-done(((bf16[8,4,8,896]{3,2,1,0:T(8,128)(2,1)}), bf16[8,4,8,896]{3,2,1,0:T(8,128)(2,1)S(1)}, u32[]{:S(2)}, u32[]{:S(2)}) %all-to-all-start) | async-done | bytes 458784 | tf_op jit(solution)/shard_map/all_to_all | solution.py:512
  52.0 0.0 copy-done.1
  52.0 8.7 %shard_map.95 = bf16[384,576]{1,0:T(8,128)(2,1)S(1)} custom-call(f32[2]{0:T(128)S(1)} %fusion.10.weights, bf16[8,4,8,896]{3,2,1,0:T(8,128)(2,1)S(1)} %all-to-all-done.block, f32[5,13,640]{2,1,0:T(8,128)S(1)} %pad.4.bank, f32[8,8]{1,0:T(8,128)S(1)} %select_reduce_fusion.coefs, bf16[1280,640]{1,0:T(8,128)(2,1)S(1)} %copy-done.1), custom_call_target="tpu_custom_call" | custom-call | flops 8000000000 | bytes 8000000 | tf_op jit(solution)/shard_map/pallas_call | solution.py:451
  60.8 0.3 reshape.35
  61.1 0.3 copy.24
  61.4 18.6 %all_to_all.23 = bf16[1,2,24,4608]{3,1,0,2:T(2,128)(2,1)S(1)} all-to-all(bf16[1,2,24,4608]{3,1,0,2:T(2,128)(2,1)S(1)} %copy.24), channel_id=1, replica_groups=mesh['gx'=8,'gy'=8,'vert'=8] {'vert'}, dimensions={2} | all-to-all | bytes 884736 | tf_op jit(solution)/shard_map/all_to_all | solution.py:532
  80.0 0.8 copy.26
  (3 shorter events, 0.0 us)
Async XLA Ops:
  0.0 21.7 %copy-start.3 = (s32[64,16]{0,1:T(8,128)S(1)}, s32[64,16]{0,1:T(8,128)}, u32[]{:S(2)}) copy-start(s32[64,16]{0,1:T(8,128)} %param.10) | copy-start | bytes 12292
  0.0 24.7 %copy-start = (f32[2,8,896]{2,1,0:T(8,128)S(1)}, f32[2,8,896]{2,1,0:T(8,128)}, u32[]{:S(2)}) copy-start(f32[2,8,896]{2,1,0:T(8,128)} %constant.63.clone.speeds_y) | copy-start | bytes 172036
  1.7 23.0 %collective-permute-start.2 = (bf16[3,8,8,896]{3,2,1,0:T(8,128)(2,1)S(1)}, bf16[3,8,8,896]{3,2,1,0:T(8,128)(2,1)S(1)}, u32[]{:S(2)}, u32[]{:S(2)}) collective-permute-start(bf16[3,8,8,896]{3,2,1,0:T(8,128)(2,1)S(1)} %get-tuple-element.13), channel_id=1, source_target_pairs={{0,8},{8,16},{16,24},{24,32},{32,40},{40,48},{48,56},{56,0},{1,9},... | collective-permute-start | bytes 1032200 | tf_op jit(solution)/shard_map/ppermute | solution.py:488
  5.7 19.0 %collective-permute-start.3 = (bf16[3,8,8,896]{3,2,1,0:T(8,128)(2,1)S(1)}, bf16[3,8,8,896]{3,2,1,0:T(8,128)(2,1)S(1)}, u32[]{:S(2)}, u32[]{:S(2)}) collective-permute-start(bf16[3,8,8,896]{3,2,1,0:T(8,128)(2,1)S(1)} %get-tuple-element.14), channel_id=1, source_target_pairs={{0,56},{8,0},{16,8},{24,16},{32,24},{40,32},{48,40},{56,48},{1,57}... | collective-permute-start | bytes 1032200 | tf_op jit(solution)/shard_map/ppermute | solution.py:489
  14.9 8.0 %collective-permute-start = (bf16[4,2,8,896]{3,2,1,0:T(8,128)(2,1)S(1)}, bf16[4,2,8,896]{3,2,1,0:T(8,128)(2,1)S(1)}, u32[]{:S(2)}, u32[]{:S(2)}) collective-permute-start(bf16[4,2,8,896]{3,2,1,0:T(8,128)(2,1)S(1)} %get-tuple-element.11), channel_id=1, source_target_pairs={{0,448},{1,449},{2,450},{3,451},{4,68},{5,69},{6,70},{7,71},{64,0}... | collective-permute-start | bytes 344072 | tf_op jit(solution)/shard_map/ppermute | solution.py:500
  17.8 5.2 %collective-permute-start.1 = (bf16[4,1,8,896]{3,2,1,0:T(8,128)(2,1)S(1)}, bf16[4,1,8,896]{3,2,1,0:T(8,128)(2,1)S(1)}, u32[]{:S(2)}, u32[]{:S(2)}) collective-permute-start(bf16[4,1,8,896]{3,2,1,0:T(8,128)(2,1)S(1)} %get-tuple-element.12), channel_id=1, source_target_pairs={{0,64},{1,65},{2,66},{3,67},{4,452},{5,453},{6,454},{7,455},{64,12... | collective-permute-start | bytes 172040 | tf_op jit(solution)/shard_map/ppermute | solution.py:501
  24.7 11.3 %copy-start.2 = (f32[5,13824]{1,0:T(8,128)S(1)}, f32[5,13824]{1,0:T(8,128)}, u32[]{:S(2)}) copy-start(f32[5,13824]{1,0:T(8,128)} %param.13) | copy-start | bytes 829444
  24.7 11.5 %copy-start.6 = (f32[13]{0:T(128)S(1)}, f32[13]{0:T(128)}, u32[]{:S(2)}) copy-start(f32[13]{0:T(128)} %constant.70) | copy-start | bytes 160
  27.4 9.1 %copy-start.5 = (s32[8,8]{1,0:T(8,128)S(1)}, s32[8,8]{1,0:T(8,128)}, u32[]{:S(2)}) copy-start(s32[8,8]{1,0:T(8,128)} %param.11) | copy-start | bytes 772
  27.4 9.1 %copy-start.7 = (f32[8]{0:T(128)S(1)}, f32[8]{0:T(128)}, u32[]{:S(2)}) copy-start(f32[8]{0:T(128)} %param.12) | copy-start | bytes 100
  27.4 9.2 %copy-start.4 = (pred[8,8,8]{2,1,0:T(8,128)(4,1)S(1)}, pred[8,8,8]{2,1,0:T(8,128)(4,1)}, u32[]{:S(2)}) copy-start(pred[8,8,8]{2,1,0:T(8,128)(4,1)} %constant.65.clone) | copy-start | bytes 1540
  27.4 24.6 %copy-start.1 = (bf16[1280,640]{1,0:T(8,128)(2,1)S(1)}, bf16[1280,640]{1,0:T(8,128)(2,1)}, u32[]{:S(2)}) copy-start(bf16[1280,640]{1,0:T(8,128)(2,1)} %constant.64.clone.back) | copy-start | bytes 4915204
  27.4 24.6 %all-to-all-start = ((bf16[8,4,8,896]{3,2,1,0:T(8,128)(2,1)}), bf16[8,4,8,896]{3,2,1,0:T(8,128)(2,1)S(1)}, u32[]{:S(2)}, u32[]{:S(2)}) async-start(bf16[8,4,8,896]{3,2,1,0:T(8,128)(2,1)} %shard_map.94), calls=%async_computation | async-start | bytes 917504 | tf_op jit(solution)/shard_map/all_to_all | solution.py:512

commit v4 on v3

--- a/solution.py
+++ b/solution.py
@@ -75,9 +75,9 @@
                     to_low[LOW_ORDER.index(q), x] = value
 
 
-def edges_kernel(flags, own, to_down, to_up):
+def edges_kernel(own, to_down, to_up):
     rows_x = own.shape[1]
-    forward = flags[0] > 0
+    forward = lax.axis_index("vert") >= lax.axis_size("vert") // 2
     for q in range(4):
         for step in range(2):
             row = jnp.where(forward, rows_x - 2 + step, 1 - step)
@@ -85,19 +85,18 @@
         to_up[q, 0] = own[q, jnp.where(forward, 0, rows_x - 1)]
 
 
-def edges(flag, own):
-    smem = pl.BlockSpec(memory_space=pltpu.SMEM)
+def edges(own):
     vmem = pl.BlockSpec(memory_space=pltpu.VMEM)
     return pl.pallas_call(
         edges_kernel,
         out_shape=[
             jax.ShapeDtypeStruct((4, count, LEVELS, WIDE), jnp.bfloat16) for count in (2, 1)
         ],
-        in_specs=[smem, vmem],
+        in_specs=[vmem],
         out_specs=[vmem] * 2,
         compiler_params=pltpu.CompilerParams(vmem_limit_bytes=8 * 1024 * 1024),
         cost_estimate=pl.CostEstimate(flops=100_000, bytes_accessed=400_000, transcendentals=0),
-    )(flag, own)
+    )(own)
 
 
 def split(raw):
@@ -119,7 +118,7 @@
     return jnp.where(flag == 1, 0.0, jnp.where(flag == 2, 0.5, 1.0)).astype(jnp.float32)
 
 
-def along_x_kernel(flags, mask, own, xup, xdn, speeds_x, part, face_x):
+def along_x_kernel(flags, mask, own, xup, xdn, speeds_x, part, face_y, face_x):
     rows_x = own.shape[1]
     forward = flags[0] > 0
 
@@ -130,6 +129,10 @@
         cells = [open_at(mask, flags[1] + pick(step), flags[2] + y) for step in range(-1, rows_x + 1)]
         for step in range(rows_x + 1):
             face_x[step, y] = jnp.minimum(cells[step], cells[step + 1])
+    for row in range(rows_x):
+        cells = [open_at(mask, flags[1] + row, flags[2] + y) for y in range(-1, 3)]
+        for face in range(3):
+            face_y[row, face] = jnp.minimum(cells[face], cells[face + 1])
 
     def tile(t, carry):
         lanes = pl.ds(pl.multiple_of(t * 128, 128), 128)
@@ -156,12 +159,8 @@
     lax.fori_loop(0, WIDE // 128, tile, 0)
 
 
-def along_y_kernel(flags, mask, part, own, low, high_, speeds_y, out, face_y):
+def along_y_kernel(face_y, part, own, low, high_, speeds_y, out):
     rows_x = own.shape[1]
-    for row in range(rows_x):
-        cells = [open_at(mask, flags[1] + row, flags[2] + y) for y in range(-1, 3)]
-        for face in range(3):
-            face_y[row, face] = jnp.minimum(cells[face], cells[face + 1])
 
     def tile(t, carry):
         lanes = pl.ds(pl.multiple_of(t * 128, 128), 128)
@@ -197,28 +196,30 @@
     vmem = pl.BlockSpec(memory_space=pltpu.VMEM)
     return pl.pallas_call(
         along_x_kernel,
-        out_shape=jax.ShapeDtypeStruct(own.shape, jnp.float32),
+        out_shape=[
+            jax.ShapeDtypeStruct(own.shape, jnp.float32),
+            jax.ShapeDtypeStruct((own.shape[1], 3), jnp.float32),
+        ],
         in_specs=[smem] * 2 + [vmem] * 4,
-        out_specs=vmem,
+        out_specs=[vmem, smem],
         scratch_shapes=[pltpu.SMEM((own.shape[1] + 1, 2), jnp.float32)],
         compiler_params=pltpu.CompilerParams(vmem_limit_bytes=8 * 1024 * 1024),
         cost_estimate=pl.CostEstimate(flops=5_000_000, bytes_accessed=1_500_000, transcendentals=0),
     )(flag, mask, own, xup, xdn, speeds_x)
 
 
-def along_y(flag, mask, part, own, low, high_, speeds_y):
+def along_y(face_y, part, own, low, high_, speeds_y):
     rows_x = own.shape[1]
     smem = pl.BlockSpec(memory_space=pltpu.SMEM)
     vmem = pl.BlockSpec(memory_space=pltpu.VMEM)
     return pl.pallas_call(
         along_y_kernel,
         out_shape=jax.ShapeDtypeStruct((rows_x, 4, LEVELS, WIDE), jnp.bfloat16),
-        in_specs=[smem] * 2 + [vmem] * 5,
+        in_specs=[smem] + [vmem] * 5,
         out_specs=vmem,
-        scratch_shapes=[pltpu.SMEM((rows_x, 3), jnp.float32)],
         compiler_params=pltpu.CompilerParams(vmem_limit_bytes=8 * 1024 * 1024),
         cost_estimate=pl.CostEstimate(flops=5_000_000, bytes_accessed=2_500_000, transcendentals=0),
-    )(flag, mask, part, own, low, high_, speeds_y)
+    )(face_y, part, own, low, high_, speeds_y)
 
 
 def small(matrix, inputs):
@@ -490,7 +491,7 @@
 
     index_x = at_v * local_vx + jnp.arange(WIDE, dtype=jnp.int32) // HALF
     speeds_x = jnp.abs(speed(index_x.astype(jnp.float32)))
-    upstream, downstream = edges(flag, own)
+    upstream, downstream = edges(own)
     send_up, send_down = [], []
     for i in range(count_x):
         for v in range(count_v):
@@ -505,8 +506,8 @@
 
     speeds_x = jnp.broadcast_to(speeds_x[None], (LEVELS, WIDE))
     speeds_y = jnp.asarray(lane_speeds())
-    part = along_x(flag, wall_mask, own, xup, xdn, speeds_x)
-    transported = along_y(flag, wall_mask, part, own, low, high_, speeds_y)
+    part, face_y = along_x(flag, wall_mask, own, xup, xdn, speeds_x)
+    transported = along_y(face_y, part, own, low, high_, speeds_y)
 
     back = jnp.asarray(split_table())
     block = lax.all_to_all(transported, "vert", split_axis=0, concat_axis=0, tiled=True)

time: 82.3 us -> 81.8 us (level)
  no operation moved by 1% of the time
where the time goes in v4:
time: 81.8 us; the launch traced here: 80.4 us
  starting transfers between devices  28 us (34%)
  blocking collectives  18.6 us (23%)
  waiting for transfers between devices  16.3 us (20%)
  Pallas kernels  13.5 us (17%)
  local copies, waits for them, and re-layouts  3.18 us (4%)
    all_to_all x1, blocking collectives, body(): lax.all_to_all(updated, 'vert', split_axis=2, concat_axis=0, tiled=True)  18.6 us
    all_to_all x1, waiting for transfers between devices, body(): lax.all_to_all(transported, 'vert', split_axis=0, concat_axis=0, tiled=True)  15.3 us
    pallas_call x1, Pallas kernels, collide(): pl.pallas_call(collide_kernel, out_shape=jax.ShapeDtypeStruct((count, PLA...  8.71 us
    all_to_all x1, starting transfers between devices, body(): lax.all_to_all(transported, 'vert', split_axis=0, concat_axis=0, tiled=True)  8.61 us
    ppermute x1, starting transfers between devices, body(): high_ = lax.ppermute(to_low, 'gy', ring(count_y, -1))  8.59 us
    ppermute x1, starting transfers between devices, body(): low = lax.ppermute(to_high, 'gy', ring(count_y, 1))  4 us
    ppermute x1, starting transfers between devices, body(): xdn = lax.ppermute(downstream, ('gx', 'vert'), send_down)  3.91 us
    ppermute x1, starting transfers between devices, body(): xup = lax.ppermute(upstream, ('gx', 'vert'), send_up)  2.86 us
  transfers between devices with their start and end apart: 5, of which 2 were waited for; matrix products, arithmetic and copies ran while one was open for 1% of the time, Pallas kernels for 3%

profile of v4, /device:TPU:7, one launch (start us, length us, event | category | flops | bytes accessed | tf_op | source)
XLA Modules:
  0.0 80.4 jit_solution(7390923712433657352)
XLA Ops:
  0.0 0.0 copy-start
  0.0 0.0 copy-start.3
  0.0 1.5 %reshape.33.raw = bf16[8,3,2,8,576]{4,3,2,1,0:T(8,128)(2,1)S(1)} reshape(bf16[8,3,2,4608]{3,2,1,0:T(2,128)(2,1)} %bitcast.10) | data formatting | bytes 884736 | tf_op jit(solution)/shard_map/reshape | solution.py:487
  1.5 0.2 shard_map.91
  1.7 4.0 %collective-permute-start.2 = (bf16[3,8,8,896]{3,2,1,0:T(8,128)(2,1)S(1)}, bf16[3,8,8,896]{3,2,1,0:T(8,128)(2,1)S(1)}, u32[]{:S(2)}, u32[]{:S(2)}) collective-permute-start(bf16[3,8,8,896]{3,2,1,0:T(8,128)(2,1)S(1)} %get-tuple-element.17), channel_id=1, source_target_pairs={{0,8},{8,16},{16,24},{24,32},{32,40},{40,48},{48,56},{56,0},{1,9},... | collective-permute-start | bytes 1032200 | tf_op jit(solution)/shard_map/ppermute | solution.py:489
  5.7 8.6 %collective-permute-start.3 = (bf16[3,8,8,896]{3,2,1,0:T(8,128)(2,1)S(1)}, bf16[3,8,8,896]{3,2,1,0:T(8,128)(2,1)S(1)}, u32[]{:S(2)}, u32[]{:S(2)}) collective-permute-start(bf16[3,8,8,896]{3,2,1,0:T(8,128)(2,1)S(1)} %get-tuple-element.18), channel_id=1, source_target_pairs={{0,56},{8,0},{16,8},{24,16},{32,24},{40,32},{48,40},{56,48},{1,57}... | collective-permute-start | bytes 1032200 | tf_op jit(solution)/shard_map/ppermute | solution.py:490
  14.3 2.9 %collective-permute-start = (bf16[4,2,8,896]{3,2,1,0:T(8,128)(2,1)S(1)}, bf16[4,2,8,896]{3,2,1,0:T(8,128)(2,1)S(1)}, u32[]{:S(2)}, u32[]{:S(2)}) collective-permute-start(bf16[4,2,8,896]{3,2,1,0:T(8,128)(2,1)S(1)} %get-tuple-element.13), channel_id=1, source_target_pairs={{0,448},{1,449},{2,450},{3,451},{4,68},{5,69},{6,70},{7,71},{64,0}... | collective-permute-start | bytes 344072 | tf_op jit(solution)/shard_map/ppermute | solution.py:501
  17.2 3.9 %collective-permute-start.1 = (bf16[4,1,8,896]{3,2,1,0:T(8,128)(2,1)S(1)}, bf16[4,1,8,896]{3,2,1,0:T(8,128)(2,1)S(1)}, u32[]{:S(2)}, u32[]{:S(2)}) collective-permute-start(bf16[4,1,8,896]{3,2,1,0:T(8,128)(2,1)S(1)} %get-tuple-element.14), channel_id=1, source_target_pairs={{0,64},{1,65},{2,66},{3,67},{4,452},{5,453},{6,454},{7,455},{64,12... | collective-permute-start | bytes 172040 | tf_op jit(solution)/shard_map/ppermute | solution.py:502
  21.2 0.0 copy-done.3
  21.2 0.1 copy.18.mask
  21.3 0.1 pad_add_fusion.flags
  21.3 1.0 %collective-permute-done.1.xdn = bf16[4,1,8,896]{3,2,1,0:T(8,128)(2,1)S(1)} collective-permute-done((bf16[4,1,8,896]{3,2,1,0:T(8,128)(2,1)S(1)}, bf16[4,1,8,896]{3,2,1,0:T(8,128)(2,1)S(1)}, u32[]{:S(2)}, u32[]{:S(2)}) %collective-permute-start.1) | collective-permute-done | bytes 57376 | tf_op jit(solution)/shard_map/ppermute | solution.py:502
  22.4 0.0 collective-permute-done.xup
  22.4 2.5 %shard_map.93 = (f32[4,8,8,896]{3,2,1,0:T(8,128)S(1)}, f32[8,3]{1,0:T(8,128)S(1)}) custom-call(s32[3]{0:T(128)S(1)} %pad_add_fusion.flags, s32[64,16]{1,0:T(8,128)S(1)} %copy.18.mask, bf16[4,8,8,896]{3,2,1,0:T(8,128)(2,1)S(1)} %get-tuple-element.12.own, bf16[4,2,8,896]{3,2,1,0:T(8,128)(2,1)S(1)} %collective-permute-done.xup, ...), custom_call_target="tpu_custom_call" | custom-call | flops 5000000 | bytes 1500000 | tf_op jit(solution)/shard_map/pallas_call | solution.py:197
  24.8 0.0 collective-permute-done.2.low
  24.9 0.0 collective-permute-done.3.high_
  24.9 0.0 copy-done
  24.9 0.0 copy-start.2
  24.9 0.0 copy-start.6
  24.9 2.1 %shard_map.94 = bf16[8,4,8,896]{3,2,1,0:T(8,128)(2,1)} custom-call(f32[8,3]{1,0:T(8,128)S(1)} %get-tuple-element.15.face_y, f32[4,8,8,896]{3,2,1,0:T(8,128)S(1)} %get-tuple-element.16.part, bf16[4,8,8,896]{3,2,1,0:T(8,128)(2,1)S(1)} %get-tuple-element.12.own, bf16[3,8,8,896]{3,2,1,0:T(8,128)(2,1)S(1)} %collective-permute-done.2.low, ...), custom_call_target="tpu_custom_call" | custom-call | flops 5000000 | bytes 2500000 | tf_op jit(solution)/shard_map/pallas_call | solution.py:215
  27.0 0.0 copy-start.5
  27.0 0.0 copy-start.7
  27.0 0.0 copy-start.4
  27.0 0.0 copy-start.1
  27.0 8.6 %all-to-all-start = ((bf16[8,4,8,896]{3,2,1,0:T(8,128)(2,1)}), bf16[8,4,8,896]{3,2,1,0:T(8,128)(2,1)S(1)}, u32[]{:S(2)}, u32[]{:S(2)}) async-start(bf16[8,4,8,896]{3,2,1,0:T(8,128)(2,1)} %shard_map.94), calls=%async_computation | async-start | bytes 917504 | tf_op jit(solution)/shard_map/all_to_all | solution.py:513
  35.6 0.0 copy-done.2
  35.6 0.1 reshape.34
  35.7 0.0 copy-done.6
  35.7 0.1 slice_multiply_fusion
  35.8 0.2 fusion.10.weights
  36.0 0.0 copy-done.5
  36.0 0.0 copy-done.7
  36.1 0.2 select_reduce_fusion.1
  36.2 0.0 copy-done.4
  36.2 0.1 select_reduce_fusion.coefs
  36.3 15.3 %all-to-all-done.block = bf16[8,4,8,896]{3,2,1,0:T(8,128)(2,1)S(1)} async-done(((bf16[8,4,8,896]{3,2,1,0:T(8,128)(2,1)}), bf16[8,4,8,896]{3,2,1,0:T(8,128)(2,1)S(1)}, u32[]{:S(2)}, u32[]{:S(2)}) %all-to-all-start) | async-done | bytes 458784 | tf_op jit(solution)/shard_map/all_to_all | solution.py:513
  51.6 0.0 copy-done.1
  51.6 8.7 %shard_map.95 = bf16[384,576]{1,0:T(8,128)(2,1)S(1)} custom-call(f32[2]{0:T(128)S(1)} %fusion.10.weights, bf16[8,4,8,896]{3,2,1,0:T(8,128)(2,1)S(1)} %all-to-all-done.block, f32[5,13,640]{2,1,0:T(8,128)S(1)} %pad.4.bank, f32[8,8]{1,0:T(8,128)S(1)} %select_reduce_fusion.coefs, bf16[1280,640]{1,0:T(8,128)(2,1)S(1)} %copy-done.1), custom_call_target="tpu_custom_call" | custom-call | flops 8000000000 | bytes 8000000 | tf_op jit(solution)/shard_map/pallas_call | solution.py:452
  60.3 0.3 reshape.35
  60.7 0.3 copy.19
  61.0 18.6 %all_to_all.23 = bf16[1,2,24,4608]{3,1,0,2:T(2,128)(2,1)S(1)} all-to-all(bf16[1,2,24,4608]{3,1,0,2:T(2,128)(2,1)S(1)} %copy.19), channel_id=1, replica_groups=mesh['gx'=8,'gy'=8,'vert'=8] {'vert'}, dimensions={2} | all-to-all | bytes 884736 | tf_op jit(solution)/shard_map/all_to_all | solution.py:533
  79.6 0.8 copy.21
  (4 shorter events, 0.1 us)
Async XLA Ops:
  0.0 24.9 %copy-start = (f32[2,8,896]{2,1,0:T(8,128)S(1)}, f32[2,8,896]{2,1,0:T(8,128)}, u32[]{:S(2)}) copy-start(f32[2,8,896]{2,1,0:T(8,128)} %constant.63.clone.speeds_y) | copy-start | bytes 172036
  0.0 21.2 %copy-start.3 = (s32[64,16]{0,1:T(8,128)S(1)}, s32[64,16]{0,1:T(8,128)}, u32[]{:S(2)}) copy-start(s32[64,16]{0,1:T(8,128)} %param.10) | copy-start | bytes 12292
  1.7 23.1 %collective-permute-start.2 = (bf16[3,8,8,896]{3,2,1,0:T(8,128)(2,1)S(1)}, bf16[3,8,8,896]{3,2,1,0:T(8,128)(2,1)S(1)}, u32[]{:S(2)}, u32[]{:S(2)}) collective-permute-start(bf16[3,8,8,896]{3,2,1,0:T(8,128)(2,1)S(1)} %get-tuple-element.17), channel_id=1, source_target_pairs={{0,8},{8,16},{16,24},{24,32},{32,40},{40,48},{48,56},{56,0},{1,9},... | collective-permute-start | bytes 1032200 | tf_op jit(solution)/shard_map/ppermute | solution.py:489
  5.7 19.2 %collective-permute-start.3 = (bf16[3,8,8,896]{3,2,1,0:T(8,128)(2,1)S(1)}, bf16[3,8,8,896]{3,2,1,0:T(8,128)(2,1)S(1)}, u32[]{:S(2)}, u32[]{:S(2)}) collective-permute-start(bf16[3,8,8,896]{3,2,1,0:T(8,128)(2,1)S(1)} %get-tuple-element.18), channel_id=1, source_target_pairs={{0,56},{8,0},{16,8},{24,16},{32,24},{40,32},{48,40},{56,48},{1,57}... | collective-permute-start | bytes 1032200 | tf_op jit(solution)/shard_map/ppermute | solution.py:490
  14.3 8.0 %collective-permute-start = (bf16[4,2,8,896]{3,2,1,0:T(8,128)(2,1)S(1)}, bf16[4,2,8,896]{3,2,1,0:T(8,128)(2,1)S(1)}, u32[]{:S(2)}, u32[]{:S(2)}) collective-permute-start(bf16[4,2,8,896]{3,2,1,0:T(8,128)(2,1)S(1)} %get-tuple-element.13), channel_id=1, source_target_pairs={{0,448},{1,449},{2,450},{3,451},{4,68},{5,69},{6,70},{7,71},{64,0}... | collective-permute-start | bytes 344072 | tf_op jit(solution)/shard_map/ppermute | solution.py:501
  17.2 5.2 %collective-permute-start.1 = (bf16[4,1,8,896]{3,2,1,0:T(8,128)(2,1)S(1)}, bf16[4,1,8,896]{3,2,1,0:T(8,128)(2,1)S(1)}, u32[]{:S(2)}, u32[]{:S(2)}) collective-permute-start(bf16[4,1,8,896]{3,2,1,0:T(8,128)(2,1)S(1)} %get-tuple-element.14), channel_id=1, source_target_pairs={{0,64},{1,65},{2,66},{3,67},{4,452},{5,453},{6,454},{7,455},{64,12... | collective-permute-start | bytes 172040 | tf_op jit(solution)/shard_map/ppermute | solution.py:502
  24.9 10.7 %copy-start.2 = (f32[5,13824]{1,0:T(8,128)S(1)}, f32[5,13824]{1,0:T(8,128)}, u32[]{:S(2)}) copy-start(f32[5,13824]{1,0:T(8,128)} %param.13) | copy-start | bytes 829444
  24.9 10.8 %copy-start.6 = (f32[13]{0:T(128)S(1)}, f32[13]{0:T(128)}, u32[]{:S(2)}) copy-start(f32[13]{0:T(128)} %constant.70) | copy-start | bytes 160
  27.0 9.1 %copy-start.5 = (s32[8,8]{1,0:T(8,128)S(1)}, s32[8,8]{1,0:T(8,128)}, u32[]{:S(2)}) copy-start(s32[8,8]{1,0:T(8,128)} %param.11) | copy-start | bytes 772
  27.0 9.1 %copy-start.7 = (f32[8]{0:T(128)S(1)}, f32[8]{0:T(128)}, u32[]{:S(2)}) copy-start(f32[8]{0:T(128)} %param.12) | copy-start | bytes 100
  27.0 9.2 %copy-start.4 = (pred[8,8,8]{2,1,0:T(8,128)(4,1)S(1)}, pred[8,8,8]{2,1,0:T(8,128)(4,1)}, u32[]{:S(2)}) copy-start(pred[8,8,8]{2,1,0:T(8,128)(4,1)} %constant.65.clone) | copy-start | bytes 1540
  27.0 24.6 %copy-start.1 = (bf16[1280,640]{1,0:T(8,128)(2,1)S(1)}, bf16[1280,640]{1,0:T(8,128)(2,1)}, u32[]{:S(2)}) copy-start(bf16[1280,640]{1,0:T(8,128)(2,1)} %constant.64.clone.back) | copy-start | bytes 4915204
  27.0 24.6 %all-to-all-start = ((bf16[8,4,8,896]{3,2,1,0:T(8,128)(2,1)}), bf16[8,4,8,896]{3,2,1,0:T(8,128)(2,1)S(1)}, u32[]{:S(2)}, u32[]{:S(2)}) async-start(bf16[8,4,8,896]{3,2,1,0:T(8,128)(2,1)} %shard_map.94), calls=%async_computation | async-start | bytes 917504 | tf_op jit(solution)/shard_map/all_to_all | solution.py:513

commit v5 on v4

--- a/solution.py
+++ b/solution.py
@@ -118,8 +118,8 @@
     return jnp.where(flag == 1, 0.0, jnp.where(flag == 2, 0.5, 1.0)).astype(jnp.float32)
 
 
-def along_x_kernel(flags, mask, own, xup, xdn, speeds_x, part, face_y, face_x):
-    rows_x = own.shape[1]
+def faces_kernel(flags, mask, face_x, face_y):
+    rows_x = face_y.shape[0]
     forward = flags[0] > 0
 
     def pick(step):
@@ -133,6 +133,29 @@
         cells = [open_at(mask, flags[1] + row, flags[2] + y) for y in range(-1, 3)]
         for face in range(3):
             face_y[row, face] = jnp.minimum(cells[face], cells[face + 1])
+
+
+def faces(flag, mask, rows_x):
+    smem = pl.BlockSpec(memory_space=pltpu.SMEM)
+    return pl.pallas_call(
+        faces_kernel,
+        out_shape=[
+            jax.ShapeDtypeStruct((rows_x + 1, 2), jnp.float32),
+            jax.ShapeDtypeStruct((rows_x, 3), jnp.float32),
+        ],
+        in_specs=[smem] * 2,
+        out_specs=[smem] * 2,
+        compiler_params=pltpu.CompilerParams(vmem_limit_bytes=8 * 1024 * 1024),
+        cost_estimate=pl.CostEstimate(flops=1_000, bytes_accessed=10_000, transcendentals=0),
+    )(flag, mask)
+
+
+def along_x_kernel(face_x, own, xup, xdn, speeds_x, part):
+    rows_x = own.shape[1]
+    forward = lax.axis_index("vert") >= lax.axis_size("vert") // 2
+
+    def pick(step):
+        return jnp.where(forward, step, rows_x - 1 - step)
 
     def tile(t, carry):
         lanes = pl.ds(pl.multiple_of(t * 128, 128), 128)
@@ -191,21 +214,17 @@
     lax.fori_loop(0, WIDE // 128, tile, 0)
 
 
-def along_x(flag, mask, own, xup, xdn, speeds_x):
+def along_x(face_x, own, xup, xdn, speeds_x):
     smem = pl.BlockSpec(memory_space=pltpu.SMEM)
     vmem = pl.BlockSpec(memory_space=pltpu.VMEM)
     return pl.pallas_call(
         along_x_kernel,
-        out_shape=[
-            jax.ShapeDtypeStruct(own.shape, jnp.float32),
-            jax.ShapeDtypeStruct((own.shape[1], 3), jnp.float32),
-        ],
-        in_specs=[smem] * 2 + [vmem] * 4,
-        out_specs=[vmem, smem],
-        scratch_shapes=[pltpu.SMEM((own.shape[1] + 1, 2), jnp.float32)],
+        out_shape=jax.ShapeDtypeStruct(own.shape, jnp.float32),
+        in_specs=[smem] + [vmem] * 4,
+        out_specs=vmem,
         compiler_params=pltpu.CompilerParams(vmem_limit_bytes=8 * 1024 * 1024),
         cost_estimate=pl.CostEstimate(flops=5_000_000, bytes_accessed=1_500_000, transcendentals=0),
-    )(flag, mask, own, xup, xdn, speeds_x)
+    )(face_x, own, xup, xdn, speeds_x)
 
 
 def along_y(face_y, part, own, low, high_, speeds_y):
@@ -506,7 +525,8 @@
 
     speeds_x = jnp.broadcast_to(speeds_x[None], (LEVELS, WIDE))
     speeds_y = jnp.asarray(lane_speeds())
-    part, face_y = along_x(flag, wall_mask, own, xup, xdn, speeds_x)
+    face_x, face_y = faces(flag, wall_mask, rows_x)
+    part = along_x(face_x, own, xup, xdn, speeds_x)
     transported = along_y(face_y, part, own, low, high_, speeds_y)
 
     back = jnp.asarray(split_table())

time: 81.8 us -> 80.7 us (0.987)
    ppermute x1, waiting for transfers between devices: 1.03 us -> 0.01 us  [body(): xdn = lax.ppermute(downstream, ('gx', 'vert'), send_down)]
    pallas_call x1 -> x2, Pallas kernels: 2.47 us -> 3.16 us  [the longest x1 1.96 us: faces(): pl.pallas_call(faces_kernel, out_shape=[jax.ShapeDtypeStruct((rows_x + 1,...]
  transfers between devices with their start and end apart: 5 -> 5, of which waited for: 2 -> 1; matrix products, arithmetic and copies ran while one was open for 1% -> 1% of each run, Pallas kernels for 3% -> 4%
where the time goes in v5:
time: 80.7 us; the launch traced here: 79.5 us
  starting transfers between devices  27.2 us (34%)
  blocking collectives  18.6 us (23%)
  waiting for transfers between devices  15.6 us (19%)
  Pallas kernels  14.2 us (18%)
  local copies, waits for them, and re-layouts  3.18 us (4%)
    all_to_all x1, blocking collectives, body(): lax.all_to_all(updated, 'vert', split_axis=2, concat_axis=0, tiled=True)  18.6 us
    all_to_all x1, waiting for transfers between devices, body(): lax.all_to_all(transported, 'vert', split_axis=0, concat_axis=0, tiled=True)  15.5 us
    pallas_call x1, Pallas kernels, collide(): pl.pallas_call(collide_kernel, out_shape=jax.ShapeDtypeStruct((count, PLA...  8.71 us
    ppermute x1, starting transfers between devices, body(): high_ = lax.ppermute(to_low, 'gy', ring(count_y, -1))  8.59 us
    all_to_all x1, starting transfers between devices, body(): lax.all_to_all(transported, 'vert', split_axis=0, concat_axis=0, tiled=True)  7.82 us
    ppermute x1, starting transfers between devices, body(): low = lax.ppermute(to_high, 'gy', ring(count_y, 1))  4 us
    ppermute x1, starting transfers between devices, body(): xdn = lax.ppermute(downstream, ('gx', 'vert'), send_down)  3.9 us
    ppermute x1, starting transfers between devices, body(): xup = lax.ppermute(upstream, ('gx', 'vert'), send_up)  2.86 us
  transfers between devices with their start and end apart: 5, of which 1 were waited for; matrix products, arithmetic and copies ran while one was open for 1% of the time, Pallas kernels for 4%

profile of v5, /device:TPU:7, one launch (start us, length us, event | category | flops | bytes accessed | tf_op | source)
XLA Modules:
  0.0 79.5 jit_solution(1807559662983286215)
XLA Ops:
  0.0 0.0 copy-start.3
  0.0 0.0 copy-start
  0.0 1.5 %reshape.33.raw = bf16[8,3,2,8,576]{4,3,2,1,0:T(8,128)(2,1)S(1)} reshape(bf16[8,3,2,4608]{3,2,1,0:T(2,128)(2,1)} %bitcast.10) | data formatting | bytes 884736 | tf_op jit(solution)/shard_map/reshape | solution.py:506
  1.5 0.2 shard_map.92
  1.7 4.0 %collective-permute-start.2 = (bf16[3,8,8,896]{3,2,1,0:T(8,128)(2,1)S(1)}, bf16[3,8,8,896]{3,2,1,0:T(8,128)(2,1)S(1)}, u32[]{:S(2)}, u32[]{:S(2)}) collective-permute-start(bf16[3,8,8,896]{3,2,1,0:T(8,128)(2,1)S(1)} %get-tuple-element.17), channel_id=1, source_target_pairs={{0,8},{8,16},{16,24},{24,32},{32,40},{40,48},{48,56},{56,0},{1,9},... | collective-permute-start | bytes 1032200 | tf_op jit(solution)/shard_map/ppermute | solution.py:508
  5.7 8.6 %collective-permute-start.3 = (bf16[3,8,8,896]{3,2,1,0:T(8,128)(2,1)S(1)}, bf16[3,8,8,896]{3,2,1,0:T(8,128)(2,1)S(1)}, u32[]{:S(2)}, u32[]{:S(2)}) collective-permute-start(bf16[3,8,8,896]{3,2,1,0:T(8,128)(2,1)S(1)} %get-tuple-element.18), channel_id=1, source_target_pairs={{0,56},{8,0},{16,8},{24,16},{32,24},{40,32},{48,40},{56,48},{1,57}... | collective-permute-start | bytes 1032200 | tf_op jit(solution)/shard_map/ppermute | solution.py:509
  14.3 2.9 %collective-permute-start = (bf16[4,2,8,896]{3,2,1,0:T(8,128)(2,1)S(1)}, bf16[4,2,8,896]{3,2,1,0:T(8,128)(2,1)S(1)}, u32[]{:S(2)}, u32[]{:S(2)}) collective-permute-start(bf16[4,2,8,896]{3,2,1,0:T(8,128)(2,1)S(1)} %get-tuple-element.15), channel_id=1, source_target_pairs={{0,448},{1,449},{2,450},{3,451},{4,68},{5,69},{6,70},{7,71},{64,0}... | collective-permute-start | bytes 344072 | tf_op jit(solution)/shard_map/ppermute | solution.py:520
  17.2 0.1 pad_add_fusion.flags
  17.3 0.0 copy-done.3
  17.3 0.1 copy.18.mask
  17.4 3.9 %collective-permute-start.1 = (bf16[4,1,8,896]{3,2,1,0:T(8,128)(2,1)S(1)}, bf16[4,1,8,896]{3,2,1,0:T(8,128)(2,1)S(1)}, u32[]{:S(2)}, u32[]{:S(2)}) collective-permute-start(bf16[4,1,8,896]{3,2,1,0:T(8,128)(2,1)S(1)} %get-tuple-element.16), channel_id=1, source_target_pairs={{0,64},{1,65},{2,66},{3,67},{4,452},{5,453},{6,454},{7,455},{64,12... | collective-permute-start | bytes 172040 | tf_op jit(solution)/shard_map/ppermute | solution.py:521
  21.3 2.0 %shard_map.91 = (f32[9,2]{1,0:T(8,128)S(1)}, f32[8,3]{1,0:T(8,128)S(1)}) custom-call(s32[3]{0:T(128)S(1)} %pad_add_fusion.flags, s32[64,16]{1,0:T(8,128)S(1)} %copy.18.mask), custom_call_target="tpu_custom_call" | custom-call | flops 1000 | bytes 10000 | tf_op jit(solution)/shard_map/pallas_call | solution.py:140
  23.3 0.0 collective-permute-done.1.xdn
  23.3 0.0 collective-permute-done.xup
  23.3 1.2 %shard_map.94.part = f32[4,8,8,896]{3,2,1,0:T(8,128)S(1)} custom-call(f32[9,2]{1,0:T(8,128)S(1)} %get-tuple-element.13.face_x, bf16[4,8,8,896]{3,2,1,0:T(8,128)(2,1)S(1)} %get-tuple-element.14.own, bf16[4,2,8,896]{3,2,1,0:T(8,128)(2,1)S(1)} %collective-permute-done.xup, bf16[4,1,8,896]{3,2,1,0:T(8,128)(2,1)S(1)} %collective-permute-done.1.xdn, ...), custom_call_target="tpu_custom_call" | custom-call | flops 5000000 | bytes 1500000 | tf_op jit(solution)/shard_map/pallas_call | solution.py:220
  24.5 0.0 collective-permute-done.2.low
  24.5 0.0 collective-permute-done.3.high_
  24.5 0.0 copy-done
  24.5 0.0 copy-start.2
  24.6 0.0 copy-start.6
  24.6 2.1 %shard_map.95 = bf16[8,4,8,896]{3,2,1,0:T(8,128)(2,1)} custom-call(f32[8,3]{1,0:T(8,128)S(1)} %get-tuple-element.12.face_y, f32[4,8,8,896]{3,2,1,0:T(8,128)S(1)} %shard_map.94.part, bf16[4,8,8,896]{3,2,1,0:T(8,128)(2,1)S(1)} %get-tuple-element.14.own, bf16[3,8,8,896]{3,2,1,0:T(8,128)(2,1)S(1)} %collective-permute-done.2.low, ...), custom_call_target="tpu_custom_call" | custom-call | flops 5000000 | bytes 2500000 | tf_op jit(solution)/shard_map/pallas_call | solution.py:234
  26.6 0.0 copy-start.5
  26.6 0.0 copy-start.7
  26.6 0.0 copy-start.4
  26.7 0.0 copy-start.1
  26.7 7.8 %all-to-all-start = ((bf16[8,4,8,896]{3,2,1,0:T(8,128)(2,1)}), bf16[8,4,8,896]{3,2,1,0:T(8,128)(2,1)S(1)}, u32[]{:S(2)}, u32[]{:S(2)}) async-start(bf16[8,4,8,896]{3,2,1,0:T(8,128)(2,1)} %shard_map.95), calls=%async_computation | async-start | bytes 917504 | tf_op jit(solution)/shard_map/all_to_all | solution.py:533
  34.5 0.0 copy-done.2
  34.5 0.1 reshape.34
  34.6 0.0 copy-done.6
  34.6 0.1 slice_multiply_fusion
  34.7 0.2 fusion.10.weights
  34.9 0.0 copy-done.5
  34.9 0.0 copy-done.7
  34.9 0.2 select_reduce_fusion.1
  35.1 0.0 copy-done.4
  35.1 0.1 select_reduce_fusion.coefs
  35.2 15.5 %all-to-all-done.block = bf16[8,4,8,896]{3,2,1,0:T(8,128)(2,1)S(1)} async-done(((bf16[8,4,8,896]{3,2,1,0:T(8,128)(2,1)}), bf16[8,4,8,896]{3,2,1,0:T(8,128)(2,1)S(1)}, u32[]{:S(2)}, u32[]{:S(2)}) %all-to-all-start) | async-done | bytes 458784 | tf_op jit(solution)/shard_map/all_to_all | solution.py:533
  50.7 0.0 copy-done.1
  50.7 8.7 %shard_map.96 = bf16[384,576]{1,0:T(8,128)(2,1)S(1)} custom-call(f32[2]{0:T(128)S(1)} %fusion.10.weights, bf16[8,4,8,896]{3,2,1,0:T(8,128)(2,1)S(1)} %all-to-all-done.block, f32[5,13,640]{2,1,0:T(8,128)S(1)} %pad.4.bank, f32[8,8]{1,0:T(8,128)S(1)} %select_reduce_fusion.coefs, bf16[1280,640]{1,0:T(8,128)(2,1)S(1)} %copy-done.1), custom_call_target="tpu_custom_call" | custom-call | flops 8000000000 | bytes 8000000 | tf_op jit(solution)/shard_map/pallas_call | solution.py:471
  59.4 0.3 reshape.35
  59.8 0.3 copy.19
  60.1 18.6 %all_to_all.23 = bf16[1,2,24,4608]{3,1,0,2:T(2,128)(2,1)S(1)} all-to-all(bf16[1,2,24,4608]{3,1,0,2:T(2,128)(2,1)S(1)} %copy.19), channel_id=1, replica_groups=mesh['gx'=8,'gy'=8,'vert'=8] {'vert'}, dimensions={2} | all-to-all | bytes 884736 | tf_op jit(solution)/shard_map/all_to_all | solution.py:553
  78.7 0.8 copy.21
  (4 shorter events, 0.1 us)
Async XLA Ops:
  0.0 17.3 %copy-start.3 = (s32[64,16]{0,1:T(8,128)S(1)}, s32[64,16]{0,1:T(8,128)}, u32[]{:S(2)}) copy-start(s32[64,16]{0,1:T(8,128)} %param.10) | copy-start | bytes 12292
  0.0 24.5 %copy-start = (f32[2,8,896]{2,1,0:T(8,128)S(1)}, f32[2,8,896]{2,1,0:T(8,128)}, u32[]{:S(2)}) copy-start(f32[2,8,896]{2,1,0:T(8,128)} %constant.63.clone.speeds_y) | copy-start | bytes 172036
  1.7 22.8 %collective-permute-start.2 = (bf16[3,8,8,896]{3,2,1,0:T(8,128)(2,1)S(1)}, bf16[3,8,8,896]{3,2,1,0:T(8,128)(2,1)S(1)}, u32[]{:S(2)}, u32[]{:S(2)}) collective-permute-start(bf16[3,8,8,896]{3,2,1,0:T(8,128)(2,1)S(1)} %get-tuple-element.17), channel_id=1, source_target_pairs={{0,8},{8,16},{16,24},{24,32},{32,40},{40,48},{48,56},{56,0},{1,9},... | collective-permute-start | bytes 1032200 | tf_op jit(solution)/shard_map/ppermute | solution.py:508
  5.7 18.8 %collective-permute-start.3 = (bf16[3,8,8,896]{3,2,1,0:T(8,128)(2,1)S(1)}, bf16[3,8,8,896]{3,2,1,0:T(8,128)(2,1)S(1)}, u32[]{:S(2)}, u32[]{:S(2)}) collective-permute-start(bf16[3,8,8,896]{3,2,1,0:T(8,128)(2,1)S(1)} %get-tuple-element.18), channel_id=1, source_target_pairs={{0,56},{8,0},{16,8},{24,16},{32,24},{40,32},{48,40},{56,48},{1,57}... | collective-permute-start | bytes 1032200 | tf_op jit(solution)/shard_map/ppermute | solution.py:509
  14.3 9.0 %collective-permute-start = (bf16[4,2,8,896]{3,2,1,0:T(8,128)(2,1)S(1)}, bf16[4,2,8,896]{3,2,1,0:T(8,128)(2,1)S(1)}, u32[]{:S(2)}, u32[]{:S(2)}) collective-permute-start(bf16[4,2,8,896]{3,2,1,0:T(8,128)(2,1)S(1)} %get-tuple-element.15), channel_id=1, source_target_pairs={{0,448},{1,449},{2,450},{3,451},{4,68},{5,69},{6,70},{7,71},{64,0}... | collective-permute-start | bytes 344072 | tf_op jit(solution)/shard_map/ppermute | solution.py:520
  17.4 5.9 %collective-permute-start.1 = (bf16[4,1,8,896]{3,2,1,0:T(8,128)(2,1)S(1)}, bf16[4,1,8,896]{3,2,1,0:T(8,128)(2,1)S(1)}, u32[]{:S(2)}, u32[]{:S(2)}) collective-permute-start(bf16[4,1,8,896]{3,2,1,0:T(8,128)(2,1)S(1)} %get-tuple-element.16), channel_id=1, source_target_pairs={{0,64},{1,65},{2,66},{3,67},{4,452},{5,453},{6,454},{7,455},{64,12... | collective-permute-start | bytes 172040 | tf_op jit(solution)/shard_map/ppermute | solution.py:521
  24.5 9.9 %copy-start.2 = (f32[5,13824]{1,0:T(8,128)S(1)}, f32[5,13824]{1,0:T(8,128)}, u32[]{:S(2)}) copy-start(f32[5,13824]{1,0:T(8,128)} %param.13) | copy-start | bytes 829444
  24.6 10.0 %copy-start.6 = (f32[13]{0:T(128)S(1)}, f32[13]{0:T(128)}, u32[]{:S(2)}) copy-start(f32[13]{0:T(128)} %constant.70) | copy-start | bytes 160
  26.6 8.3 %copy-start.5 = (s32[8,8]{1,0:T(8,128)S(1)}, s32[8,8]{1,0:T(8,128)}, u32[]{:S(2)}) copy-start(s32[8,8]{1,0:T(8,128)} %param.11) | copy-start | bytes 772
  26.6 8.3 %copy-start.7 = (f32[8]{0:T(128)S(1)}, f32[8]{0:T(128)}, u32[]{:S(2)}) copy-start(f32[8]{0:T(128)} %param.12) | copy-start | bytes 100
  26.6 8.4 %copy-start.4 = (pred[8,8,8]{2,1,0:T(8,128)(4,1)S(1)}, pred[8,8,8]{2,1,0:T(8,128)(4,1)}, u32[]{:S(2)}) copy-start(pred[8,8,8]{2,1,0:T(8,128)(4,1)} %constant.65.clone) | copy-start | bytes 1540
  26.7 24.1 %copy-start.1 = (bf16[1280,640]{1,0:T(8,128)(2,1)S(1)}, bf16[1280,640]{1,0:T(8,128)(2,1)}, u32[]{:S(2)}) copy-start(bf16[1280,640]{1,0:T(8,128)(2,1)} %constant.64.clone.back) | copy-start | bytes 4915204
  26.7 24.1 %all-to-all-start = ((bf16[8,4,8,896]{3,2,1,0:T(8,128)(2,1)}), bf16[8,4,8,896]{3,2,1,0:T(8,128)(2,1)S(1)}, u32[]{:S(2)}, u32[]{:S(2)}) async-start(bf16[8,4,8,896]{3,2,1,0:T(8,128)(2,1)} %shard_map.95), calls=%async_computation | async-start | bytes 917504 | tf_op jit(solution)/shard_map/all_to_all | solution.py:533

commit v6 on v5

--- a/solution.py
+++ b/solution.py
@@ -435,15 +435,22 @@
     prepare_all(4, 4, mixed)
     for start, width in chunks:
         loss = product(4, start, width)
+        keep = min(width, PLANE - start)
+        values = []
         for cell in range(cells):
             at_rows = pl.ds(cell * per_cell, per_cell)
-            keep = min(width, PLANE - start)
             fields = g[at_rows, pl.ds(start, width)].astype(jnp.float32)
             part = loss[cell * per_cell : (cell + 1) * per_cell]
-            value = fields + weights[cell] * (
-                gain[at_rows, pl.ds(start, width)] - fields * part
+            values.append(
+                fields
+                + weights[cell] * (gain[at_rows, pl.ds(start, width)] - fields * part)
             )
-            out[at_rows, pl.ds(start, keep)] = value[:, :keep].astype(jnp.bfloat16)
+        for a in range(VX):
+            both = jnp.concatenate(
+                [value[a * LEVELS : (a + 1) * LEVELS, :keep] for value in values], axis=0
+            )
+            at_rows = pl.ds(a * cells * LEVELS, cells * LEVELS)
+            out[at_rows, pl.ds(start, keep)] = both.astype(jnp.bfloat16)
 
 
 def resident_kernel(source, out, sem):
@@ -549,8 +556,9 @@
     updated = collide(
         collide_step * own_open, block, bank, coefs, back
     )
-    updated = updated.reshape(1, 2, VX, row_width)
-    return lax.all_to_all(updated, "vert", split_axis=2, concat_axis=0, tiled=True)
+    updated = updated.reshape(VX, 2, row_width)
+    result = lax.all_to_all(updated, "vert", split_axis=0, concat_axis=0, tiled=True)
+    return result.reshape(rows_x, local_vx, 2, row_width).transpose(0, 2, 1, 3)
 
 
 def solution(mesh):

time: 80.7 us -> 80.5 us (level)
  no operation moved by 1% of the time
where the time goes in v6:
time: 80.5 us; the launch traced here: 79.3 us
  starting transfers between devices  27.2 us (34%)
  blocking collectives  18.6 us (23%)
  waiting for transfers between devices  15.6 us (19%)
  Pallas kernels  14.2 us (18%)
  local copies, waits for them, and re-layouts  3.04 us (4%)
    all_to_all x1, blocking collectives, body(): lax.all_to_all(updated, 'vert', split_axis=0, concat_axis=0, tiled=True)  18.6 us
    all_to_all x1, waiting for transfers between devices, body(): lax.all_to_all(transported, 'vert', split_axis=0, concat_axis=0, tiled=True)  15.5 us
    pallas_call x1, Pallas kernels, collide(): pl.pallas_call(collide_kernel, out_shape=jax.ShapeDtypeStruct((count, PLA...  8.71 us
    ppermute x1, starting transfers between devices, body(): high_ = lax.ppermute(to_low, 'gy', ring(count_y, -1))  8.59 us
    all_to_all x1, starting transfers between devices, body(): lax.all_to_all(transported, 'vert', split_axis=0, concat_axis=0, tiled=True)  7.82 us
    ppermute x1, starting transfers between devices, body(): low = lax.ppermute(to_high, 'gy', ring(count_y, 1))  4 us
    ppermute x1, starting transfers between devices, body(): xdn = lax.ppermute(downstream, ('gx', 'vert'), send_down)  3.9 us
    ppermute x1, starting transfers between devices, body(): xup = lax.ppermute(upstream, ('gx', 'vert'), send_up)  2.86 us
  transfers between devices with their start and end apart: 5, of which 1 were waited for; matrix products, arithmetic and copies ran while one was open for 1% of the time, Pallas kernels for 4%

profile of v6, /device:TPU:7, one launch (start us, length us, event | category | flops | bytes accessed | tf_op | source)
XLA Modules:
  0.0 79.3 jit_solution(12279065876146046364)
XLA Ops:
  0.0 0.0 copy-start.3
  0.0 0.0 copy-start
  0.0 1.5 %reshape.36.raw = bf16[8,3,2,8,576]{4,3,2,1,0:T(8,128)(2,1)S(1)} reshape(bf16[8,3,2,4608]{3,2,1,0:T(2,128)(2,1)} %bitcast.8) | data formatting | bytes 884736 | tf_op jit(solution)/shard_map/reshape | solution.py:513
  1.5 0.2 shard_map.92
  1.7 4.0 %collective-permute-start.2 = (bf16[3,8,8,896]{3,2,1,0:T(8,128)(2,1)S(1)}, bf16[3,8,8,896]{3,2,1,0:T(8,128)(2,1)S(1)}, u32[]{:S(2)}, u32[]{:S(2)}) collective-permute-start(bf16[3,8,8,896]{3,2,1,0:T(8,128)(2,1)S(1)} %get-tuple-element.17), channel_id=1, source_target_pairs={{0,8},{8,16},{16,24},{24,32},{32,40},{40,48},{48,56},{56,0},{1,9},... | collective-permute-start | bytes 1032200 | tf_op jit(solution)/shard_map/ppermute | solution.py:515
  5.7 8.6 %collective-permute-start.3 = (bf16[3,8,8,896]{3,2,1,0:T(8,128)(2,1)S(1)}, bf16[3,8,8,896]{3,2,1,0:T(8,128)(2,1)S(1)}, u32[]{:S(2)}, u32[]{:S(2)}) collective-permute-start(bf16[3,8,8,896]{3,2,1,0:T(8,128)(2,1)S(1)} %get-tuple-element.18), channel_id=1, source_target_pairs={{0,56},{8,0},{16,8},{24,16},{32,24},{40,32},{48,40},{56,48},{1,57}... | collective-permute-start | bytes 1032200 | tf_op jit(solution)/shard_map/ppermute | solution.py:516
  14.3 2.9 %collective-permute-start = (bf16[4,2,8,896]{3,2,1,0:T(8,128)(2,1)S(1)}, bf16[4,2,8,896]{3,2,1,0:T(8,128)(2,1)S(1)}, u32[]{:S(2)}, u32[]{:S(2)}) collective-permute-start(bf16[4,2,8,896]{3,2,1,0:T(8,128)(2,1)S(1)} %get-tuple-element.15), channel_id=1, source_target_pairs={{0,448},{1,449},{2,450},{3,451},{4,68},{5,69},{6,70},{7,71},{64,0}... | collective-permute-start | bytes 344072 | tf_op jit(solution)/shard_map/ppermute | solution.py:527
  17.2 0.1 pad_add_fusion.flags
  17.3 0.0 copy-done.3
  17.3 0.1 copy.12.mask
  17.4 3.9 %collective-permute-start.1 = (bf16[4,1,8,896]{3,2,1,0:T(8,128)(2,1)S(1)}, bf16[4,1,8,896]{3,2,1,0:T(8,128)(2,1)S(1)}, u32[]{:S(2)}, u32[]{:S(2)}) collective-permute-start(bf16[4,1,8,896]{3,2,1,0:T(8,128)(2,1)S(1)} %get-tuple-element.16), channel_id=1, source_target_pairs={{0,64},{1,65},{2,66},{3,67},{4,452},{5,453},{6,454},{7,455},{64,12... | collective-permute-start | bytes 172040 | tf_op jit(solution)/shard_map/ppermute | solution.py:528
  21.3 2.0 %shard_map.91 = (f32[9,2]{1,0:T(8,128)S(1)}, f32[8,3]{1,0:T(8,128)S(1)}) custom-call(s32[3]{0:T(128)S(1)} %pad_add_fusion.flags, s32[64,16]{1,0:T(8,128)S(1)} %copy.12.mask), custom_call_target="tpu_custom_call" | custom-call | flops 1000 | bytes 10000 | tf_op jit(solution)/shard_map/pallas_call | solution.py:140
  23.3 0.0 collective-permute-done.1.xdn
  23.3 0.0 collective-permute-done.xup
  23.3 1.2 %shard_map.94.part = f32[4,8,8,896]{3,2,1,0:T(8,128)S(1)} custom-call(f32[9,2]{1,0:T(8,128)S(1)} %get-tuple-element.13.face_x, bf16[4,8,8,896]{3,2,1,0:T(8,128)(2,1)S(1)} %get-tuple-element.14.own, bf16[4,2,8,896]{3,2,1,0:T(8,128)(2,1)S(1)} %collective-permute-done.xup, bf16[4,1,8,896]{3,2,1,0:T(8,128)(2,1)S(1)} %collective-permute-done.1.xdn, ...), custom_call_target="tpu_custom_call" | custom-call | flops 5000000 | bytes 1500000 | tf_op jit(solution)/shard_map/pallas_call | solution.py:220
  24.5 0.0 collective-permute-done.2.low
  24.5 0.0 collective-permute-done.3.high_
  24.5 0.0 copy-done
  24.5 0.0 copy-start.2
  24.6 0.0 copy-start.6
  24.6 2.1 %shard_map.95 = bf16[8,4,8,896]{3,2,1,0:T(8,128)(2,1)} custom-call(f32[8,3]{1,0:T(8,128)S(1)} %get-tuple-element.12.face_y, f32[4,8,8,896]{3,2,1,0:T(8,128)S(1)} %shard_map.94.part, bf16[4,8,8,896]{3,2,1,0:T(8,128)(2,1)S(1)} %get-tuple-element.14.own, bf16[3,8,8,896]{3,2,1,0:T(8,128)(2,1)S(1)} %collective-permute-done.2.low, ...), custom_call_target="tpu_custom_call" | custom-call | flops 5000000 | bytes 2500000 | tf_op jit(solution)/shard_map/pallas_call | solution.py:234
  26.6 0.0 copy-start.5
  26.6 0.0 copy-start.7
  26.6 0.0 copy-start.4
  26.7 0.0 copy-start.1
  26.7 7.8 %all-to-all-start = ((bf16[8,4,8,896]{3,2,1,0:T(8,128)(2,1)}), bf16[8,4,8,896]{3,2,1,0:T(8,128)(2,1)S(1)}, u32[]{:S(2)}, u32[]{:S(2)}) async-start(bf16[8,4,8,896]{3,2,1,0:T(8,128)(2,1)} %shard_map.95), calls=%async_computation | async-start | bytes 917504 | tf_op jit(solution)/shard_map/all_to_all | solution.py:540
  34.5 0.0 copy-done.2
  34.5 0.1 reshape.37
  34.6 0.0 copy-done.6
  34.6 0.1 slice_multiply_fusion
  34.7 0.2 fusion.10.weights
  34.9 0.0 copy-done.5
  34.9 0.0 copy-done.7
  34.9 0.2 select_reduce_fusion.1
  35.1 0.0 copy-done.4
  35.1 0.1 select_reduce_fusion.coefs
  35.2 15.5 %all-to-all-done.block = bf16[8,4,8,896]{3,2,1,0:T(8,128)(2,1)S(1)} async-done(((bf16[8,4,8,896]{3,2,1,0:T(8,128)(2,1)}), bf16[8,4,8,896]{3,2,1,0:T(8,128)(2,1)S(1)}, u32[]{:S(2)}, u32[]{:S(2)}) %all-to-all-start) | async-done | bytes 458784 | tf_op jit(solution)/shard_map/all_to_all | solution.py:540
  50.7 0.0 copy-done.1
  50.7 8.7 %shard_map.96 = bf16[384,576]{1,0:T(8,128)(2,1)S(1)} custom-call(f32[2]{0:T(128)S(1)} %fusion.10.weights, bf16[8,4,8,896]{3,2,1,0:T(8,128)(2,1)S(1)} %all-to-all-done.block, f32[5,13,640]{2,1,0:T(8,128)S(1)} %pad.4.bank, f32[8,8]{1,0:T(8,128)S(1)} %select_reduce_fusion.coefs, bf16[1280,640]{1,0:T(8,128)(2,1)S(1)} %copy-done.1), custom_call_target="tpu_custom_call" | custom-call | flops 8000000000 | bytes 8000000 | tf_op jit(solution)/shard_map/pallas_call | solution.py:478
  59.4 0.5 reshape.38
  60.0 18.6 %all_to_all.10 = bf16[24,2,4608]{2,1,0:T(2,128)(2,1)S(1)} all-to-all(bf16[24,2,4608]{2,1,0:T(2,128)(2,1)S(1)} %reshape.38), channel_id=1, replica_groups=mesh['gx'=8,'gy'=8,'vert'=8] {'vert'}, dimensions={0} | all-to-all | bytes 884736 | tf_op jit(solution)/shard_map/all_to_all | solution.py:560
  78.6 0.8 copy.14
  (4 shorter events, 0.1 us)
Async XLA Ops:
  0.0 17.3 %copy-start.3 = (s32[64,16]{0,1:T(8,128)S(1)}, s32[64,16]{0,1:T(8,128)}, u32[]{:S(2)}) copy-start(s32[64,16]{0,1:T(8,128)} %param.10) | copy-start | bytes 12292
  0.0 24.5 %copy-start = (f32[2,8,896]{2,1,0:T(8,128)S(1)}, f32[2,8,896]{2,1,0:T(8,128)}, u32[]{:S(2)}) copy-start(f32[2,8,896]{2,1,0:T(8,128)} %constant.63.clone.speeds_y) | copy-start | bytes 172036
  1.7 22.8 %collective-permute-start.2 = (bf16[3,8,8,896]{3,2,1,0:T(8,128)(2,1)S(1)}, bf16[3,8,8,896]{3,2,1,0:T(8,128)(2,1)S(1)}, u32[]{:S(2)}, u32[]{:S(2)}) collective-permute-start(bf16[3,8,8,896]{3,2,1,0:T(8,128)(2,1)S(1)} %get-tuple-element.17), channel_id=1, source_target_pairs={{0,8},{8,16},{16,24},{24,32},{32,40},{40,48},{48,56},{56,0},{1,9},... | collective-permute-start | bytes 1032200 | tf_op jit(solution)/shard_map/ppermute | solution.py:515
  5.7 18.8 %collective-permute-start.3 = (bf16[3,8,8,896]{3,2,1,0:T(8,128)(2,1)S(1)}, bf16[3,8,8,896]{3,2,1,0:T(8,128)(2,1)S(1)}, u32[]{:S(2)}, u32[]{:S(2)}) collective-permute-start(bf16[3,8,8,896]{3,2,1,0:T(8,128)(2,1)S(1)} %get-tuple-element.18), channel_id=1, source_target_pairs={{0,56},{8,0},{16,8},{24,16},{32,24},{40,32},{48,40},{56,48},{1,57}... | collective-permute-start | bytes 1032200 | tf_op jit(solution)/shard_map/ppermute | solution.py:516
  14.3 9.0 %collective-permute-start = (bf16[4,2,8,896]{3,2,1,0:T(8,128)(2,1)S(1)}, bf16[4,2,8,896]{3,2,1,0:T(8,128)(2,1)S(1)}, u32[]{:S(2)}, u32[]{:S(2)}) collective-permute-start(bf16[4,2,8,896]{3,2,1,0:T(8,128)(2,1)S(1)} %get-tuple-element.15), channel_id=1, source_target_pairs={{0,448},{1,449},{2,450},{3,451},{4,68},{5,69},{6,70},{7,71},{64,0}... | collective-permute-start | bytes 344072 | tf_op jit(solution)/shard_map/ppermute | solution.py:527
  17.4 5.9 %collective-permute-start.1 = (bf16[4,1,8,896]{3,2,1,0:T(8,128)(2,1)S(1)}, bf16[4,1,8,896]{3,2,1,0:T(8,128)(2,1)S(1)}, u32[]{:S(2)}, u32[]{:S(2)}) collective-permute-start(bf16[4,1,8,896]{3,2,1,0:T(8,128)(2,1)S(1)} %get-tuple-element.16), channel_id=1, source_target_pairs={{0,64},{1,65},{2,66},{3,67},{4,452},{5,453},{6,454},{7,455},{64,12... | collective-permute-start | bytes 172040 | tf_op jit(solution)/shard_map/ppermute | solution.py:528
  24.5 9.9 %copy-start.2 = (f32[5,13824]{1,0:T(8,128)S(1)}, f32[5,13824]{1,0:T(8,128)}, u32[]{:S(2)}) copy-start(f32[5,13824]{1,0:T(8,128)} %param.13) | copy-start | bytes 829444
  24.6 10.0 %copy-start.6 = (f32[13]{0:T(128)S(1)}, f32[13]{0:T(128)}, u32[]{:S(2)}) copy-start(f32[13]{0:T(128)} %constant.70) | copy-start | bytes 160
  26.6 8.3 %copy-start.5 = (s32[8,8]{1,0:T(8,128)S(1)}, s32[8,8]{1,0:T(8,128)}, u32[]{:S(2)}) copy-start(s32[8,8]{1,0:T(8,128)} %param.11) | copy-start | bytes 772
  26.6 8.3 %copy-start.7 = (f32[8]{0:T(128)S(1)}, f32[8]{0:T(128)}, u32[]{:S(2)}) copy-start(f32[8]{0:T(128)} %param.12) | copy-start | bytes 100
  26.6 8.4 %copy-start.4 = (pred[8,8,8]{2,1,0:T(8,128)(4,1)S(1)}, pred[8,8,8]{2,1,0:T(8,128)(4,1)}, u32[]{:S(2)}) copy-start(pred[8,8,8]{2,1,0:T(8,128)(4,1)} %constant.65.clone) | copy-start | bytes 1540
  26.7 24.1 %copy-start.1 = (bf16[1280,640]{1,0:T(8,128)(2,1)S(1)}, bf16[1280,640]{1,0:T(8,128)(2,1)}, u32[]{:S(2)}) copy-start(bf16[1280,640]{1,0:T(8,128)(2,1)} %constant.64.clone.back) | copy-start | bytes 4915204
  26.7 24.1 %all-to-all-start = ((bf16[8,4,8,896]{3,2,1,0:T(8,128)(2,1)}), bf16[8,4,8,896]{3,2,1,0:T(8,128)(2,1)S(1)}, u32[]{:S(2)}, u32[]{:S(2)}) async-start(bf16[8,4,8,896]{3,2,1,0:T(8,128)(2,1)} %shard_map.95), calls=%async_computation | async-start | bytes 917504 | tf_op jit(solution)/shard_map/all_to_all | solution.py:540
